TPU v7x, 512 devices: a whole 4x4x16 slice. The times are simulated.
512 devices in a mesh: board: 32 (over z, y_lo), depth: 4 (over y_hi, core), hand: 4 (over x).
Axes of the slice: x: 4, y: 4 (y_hi: 2, y_lo: 2; y = y_hi * 2 + y_lo), z: 16, core: 2. Of those that a mesh axis runs over, the one named last changes fastest.
Arguments:
- reach: bfloat16 [256, 1536, 1024], P('board', 'hand', 'depth'), may hold values from 0 to 1
- payoff: bfloat16 [1024, 1024], P('depth'), may hold values from -2.670288e-05 to 2.670288e-05
- board_cards: int32 [256, 5], P('board'), may hold values from 0 to 51, as said below
- hand_rank: int32 [256, 1326], P('board'), may hold values from 0 to 7461
- logits: float32 [1536, 1024], P('hand', 'depth'), may hold values from -8 to 310, as said below
- action_counts: int32 [4, 64], replicated, may hold values from 2 to 4
- parent_seq: int32 [4, 64], replicated, may hold values from 0 to 253, as said below
Outputs:
- log_policy: float32 [1536, 1024], P('hand', 'depth')
- parent_values: float32 [1536, 1024], P('hand', 'depth')
Inputs may be any that keep to these rules, and one draw needn't show every extreme that they name: `board_cards`: each row holds five different cards. `logits`: entries are finite; in some draws a few scores are very large. `parent_seq`: each entry names a legal action slot of the level above: its remainder modulo 4 is 0 or 1.
All inputs are finite; a program needn't handle non-finite values.
Results may differ from a plain program's by a relative error of at most 0.0003.
Values may be sent and summed in bfloat16 or wider, within the bound.
A program may use at most 64 MiB of HBM per device.

v0:
```python
import jax
import jax.numpy as jnp
import numpy as np
from jax import lax
from jax.sharding import PartitionSpec as P

CARDS = 52
HANDS = 1326
ACT = 4


def passed_along(array, axis, by):
    peers = lax.axis_size(axis)
    pairs = [(i, i + by) for i in range(peers) if 0 <= i + by < peers]
    return lax.ppermute(array, axis, pairs)


def hand_table(slots):
    first, second = np.triu_indices(CARDS, 1)
    pad = slots - first.shape[0]
    first = np.concatenate([first, np.full(pad, -1)])
    second = np.concatenate([second, np.full(pad, -2)])
    return (jnp.asarray(first, jnp.int32), jnp.asarray(second, jnp.int32))


def hand_valid(cards, first, second, real):
    hit_first = jnp.any(first[None, :, None] == cards[:, None, :], axis=2)
    hit_second = jnp.any(second[None, :, None] == cards[:, None, :], axis=2)
    return real[None, :] & jnp.logical_not(hit_first) & jnp.logical_not(hit_second)


def showdown_block(
    valid_rows, valid_cols, rank_rows, rank_cols, first_rows, second_rows, first_cols, second_cols
):
    apart = (first_rows[:, None] != first_cols[None, :]) & (
        first_rows[:, None] != second_cols[None, :]
    )
    apart = (
        apart
        & (second_rows[:, None] != first_cols[None, :])
        & (second_rows[:, None] != second_cols[None, :])
    )
    signs = jnp.sign(rank_rows[:, :, None] - rank_cols[:, None, :]).astype(jnp.float32)
    live = valid_rows[:, :, None] & valid_cols[:, None, :] & apart[None]
    return jnp.where(live, signs, jnp.float32(0.0)).astype(jnp.bfloat16)


def prox_level(scores, counts, parents):
    rows = scores.shape[0]
    levels_seq = scores.shape[1]
    grouped = scores.reshape(rows, levels_seq // ACT, ACT)
    legal = jnp.arange(ACT, dtype=jnp.int32)[None, :] < counts[:, None]
    masked = jnp.where(legal[None], grouped, -jnp.inf)
    top = jnp.max(masked, axis=2, keepdims=True)
    total = jnp.sum(jnp.exp(masked - top), axis=2, keepdims=True)
    value = top + jnp.log(total)
    policy = jnp.where(legal[None], grouped - value, jnp.float32(0.0)).reshape(rows, levels_seq)
    owner = (parents[:, None] == jnp.arange(levels_seq, dtype=jnp.int32)[None, :]).astype(
        jnp.float32
    )
    passed = jnp.dot(value[:, :, 0], owner, precision=lax.Precision.HIGHEST)
    return (policy, passed)


def local(reach, payoff, board_cards, hand_rank, logits, action_counts, parent_seq):
    local_hands = reach.shape[1]
    all_hands = local_hands * lax.axis_size("hand")
    first, second = hand_table(all_hands)
    real = jnp.arange(all_hands, dtype=jnp.int32) < HANDS
    valid_all = hand_valid(board_cards, first, second, real)
    ranks_all = jnp.pad(hand_rank, ((0, 0), (0, all_hands - hand_rank.shape[1])))
    offset = lax.axis_index("hand") * local_hands
    first_rows = lax.dynamic_slice_in_dim(first, offset, local_hands)
    second_rows = lax.dynamic_slice_in_dim(second, offset, local_hands)
    valid_rows = lax.dynamic_slice_in_dim(valid_all, offset, local_hands, 1)
    rank_rows = lax.dynamic_slice_in_dim(ranks_all, offset, local_hands, 1)
    empty = jnp.zeros((reach.shape[0], local_hands, reach.shape[2]), jnp.float32)
    piece = lax.all_gather(reach, "hand", axis=1, tiled=True)
    width = piece.shape[1]
    block = showdown_block(
        valid_rows,
        lax.slice_in_dim(valid_all, 0, width, axis=1),
        rank_rows,
        ranks_all,
        first_rows,
        second_rows,
        lax.slice_in_dim(first, 0, width, axis=0),
        lax.slice_in_dim(second, 0, width, axis=0),
    )
    counter = empty + jnp.einsum("bhk,bks->bhs", block, piece, preferred_element_type=jnp.float32)
    payoff_wide = payoff.astype(jnp.float32)
    partial_value = jnp.einsum("bhs,sx->hx", counter, payoff_wide, precision=lax.Precision.HIGHEST)
    level_part = lax.psum_scatter(partial_value, "depth", scatter_dimension=1, tiled=True)
    gradient = lax.psum(level_part, "board")
    level = lax.axis_index("depth")
    levels = lax.axis_size("depth")
    counts = lax.dynamic_index_in_dim(action_counts, level, 0, False)
    parents = lax.dynamic_index_in_dim(parent_seq, level, 0, False)
    center = logits + gradient
    incoming = jnp.zeros_like(center)
    for step in range(levels - 1):
        policy, passed = prox_level(center + incoming, counts, parents)
        incoming = passed_along(passed, "depth", -1)
    policy, passed = prox_level(center + incoming, counts, parents)
    return (policy, passed)


def solution(mesh):
    return jax.shard_map(
        local,
        mesh=mesh,
        in_specs=(
            P("board", "hand", "depth"),
            P("depth", None),
            P("board", None),
            P("board", None),
            P("hand", "depth"),
            P(),
            P(),
        ),
        out_specs=(P("hand", "depth"), P("hand", "depth")),
        check_vma=False,
    )
```

profile of v0, /device:TPU:1, one launch (start us, length us, event | category | flops | bytes accessed | tf_op | source)
XLA Modules:
  0.0 461.4 jit_solution(2043794717635994824)
XLA Ops:
  7.2 0.7 all-gather.2.cloned.1.call-update
  8.0 0.8 dynamic_slice.24
  8.7 0.8 dynamic_slice.25
  9.5 0.8 copy.16
  10.3 0.8 pad.4
  11.1 0.8 compare_reduce_fusion.1
  12.0 0.7 constant_dynamic-slice_fusion.1
  12.7 1.6 compare_and_fusion
  14.3 74.4 %all-gather.2.cloned.1.call-done = bf16[8,1536,256]{2,1,0:T(8,128)(2,1)} async-done(((bf16[8,384,256]{2,1,0:T(8,128)(2,1)}), bf16[8,1536,256]{2,1,0:T(8,128)(2,1)}) %all-gather.2.cloned.1.call-update) | async-done | bytes 6291472 | tf_op jit(solution)/shard_map/all_gather | solution.py:78
  88.8 8.9 %fusion.4 = f32[384,256]{1,0:T(8,128)S(1)} fusion(bf16[8,1536,256]{2,1,0:T(8,128)(2,1)} %all-gather.2.cloned.1.call-done, s32[8,1536]{1,0:T(8,128)S(1)} %pad.4, s32[8,384]{1,0:T(8,128)S(1)} %constant_dynamic-slice_fusion.1, pred[384,1536]{1,0:T(8,128)(4,1)S(1)} %compare_and_fusion, pred[8,1536]{1,0:T(8,128)(4,1)S(1)} %not_and_fusion, ...), kind=kOutput, calls=%fused_computation.6 | convolution fusion | flops 2448949248 | bytes 7351296 | tf_op jit(solution)/shard_map/bhk,bks->bhs/dot_general | solution.py:90
  97.7 1.9 fusion.22
  99.7 51.4 %reduce-scatter.2.cloned.1.call-done = f32[384,256]{1,0:T(8,128)} async-done(((f32[384,1024]{1,0:T(8,128)}), f32[384,256]{1,0:T(8,128)}) %reduce-scatter.2.cloned.1.call-update) | async-done | bytes 393232 | tf_op jit(solution)/shard_map/reduce_scatter | solution.py:93
  151.1 0.7 fusion.19
  151.9 240.6 %all-reduce.3.cloned.1.call-done = f32[384,256]{1,0:T(8,128)} async-done(((f32[384,256]{1,0:T(8,128)}), f32[384,256]{1,0:T(8,128)}) %all-reduce.3.cloned.1.call-update) | async-done | bytes 393232 | tf_op jit(solution)/shard_map/psum | solution.py:94
  392.5 1.0 add.58
  394.1 0.4 exponential_reduce_fusion.3
  394.5 0.4 fusion.11
  394.9 24.4 %collective-permute-start = (f32[384,256]{1,0:T(8,128)S(1)}, f32[384,256]{1,0:T(8,128)S(1)}, u32[]{:S(2)}, u32[]{:S(2)}) collective-permute-start(f32[384,256]{1,0:T(8,128)S(1)} %fusion.11), channel_id=1, source_target_pairs={{4,0},{8,4},{12,8},{5,1},{9,5},{13,9},{6,2},{10,6},{14,10},{7,3},{... | collective-permute-start | bytes 1179656 | tf_op jit(solution)/shard_map/ppermute | solution.py:15
  419.3 8.0 %collective-permute-done = f32[384,256]{1,0:T(8,128)S(1)} collective-permute-done((f32[384,256]{1,0:T(8,128)S(1)}, f32[384,256]{1,0:T(8,128)S(1)}, u32[]{:S(2)}, u32[]{:S(2)}) %collective-permute-start) | collective-permute-done | bytes 393248 | tf_op jit(solution)/shard_map/ppermute | solution.py:15
  427.6 0.3 select_reduce_fusion.2
  428.0 0.4 exponential_reduce_fusion.2
  428.4 0.4 fusion.8
  428.8 2.1 collective-permute-start.1
  430.9 8.5 %collective-permute-done.1 = f32[384,256]{1,0:T(8,128)S(1)} collective-permute-done((f32[384,256]{1,0:T(8,128)S(1)}, f32[384,256]{1,0:T(8,128)S(1)}, u32[]{:S(2)}, u32[]{:S(2)}) %collective-permute-start.1) | collective-permute-done | bytes 393248 | tf_op jit(solution)/shard_map/ppermute | solution.py:15
  439.7 0.3 select_reduce_fusion.1
  440.1 0.4 exponential_reduce_fusion.1
  440.5 0.4 fusion.5
  440.9 1.9 collective-permute-start.2
  443.1 8.4 %collective-permute-done.2 = f32[384,256]{1,0:T(8,128)S(1)} collective-permute-done((f32[384,256]{1,0:T(8,128)S(1)}, f32[384,256]{1,0:T(8,128)S(1)}, u32[]{:S(2)}, u32[]{:S(2)}) %collective-permute-start.2) | collective-permute-done | bytes 393248 | tf_op jit(solution)/shard_map/ppermute | solution.py:15
  452.1 0.4 exponential_reduce_fusion
  452.6 1.1 fusion.14
  454.1 0.8 subtract_select_fusion
  (35 shorter events, 2.9 us)
Async XLA Ops:
  7.2 90.5 %copy-start = (bf16[256,1024]{1,0:T(8,128)(2,1)S(1)}, bf16[256,1024]{1,0:T(8,128)(2,1)}, u32[]{:S(2)}) copy-start(bf16[256,1024]{1,0:T(8,128)(2,1)} %param.10) | copy-start | bytes 1572868
  7.2 81.6 %all-gather.2.cloned.1.call-start = ((), (), s32[]{:S(2)}) async-start(), calls=%async_computation.1 | async-start | bytes 7864320 | tf_op jit(solution)/shard_map/all_gather | solution.py:78
  7.9 143.2 %reduce-scatter.2.cloned.1.call-start = ((), (), s32[]{:S(2)}) async-start(), calls=%async_computation.2 | async-start | bytes 1966080 | tf_op jit(solution)/shard_map/reduce_scatter | solution.py:93
  14.3 378.1 %copy-start.1 = (f32[384,256]{1,0:T(8,128)S(1)}, f32[384,256]{1,0:T(8,128)}, u32[]{:S(2)}) copy-start(f32[384,256]{1,0:T(8,128)} %param.13) | copy-start | bytes 1179652
  99.6 292.8 %all-reduce.3.cloned.1.call-start = ((), (), s32[]{:S(2)}) async-start(), calls=%async_computation.3 | async-start | bytes 786432 | tf_op jit(solution)/shard_map/psum | solution.py:94
  394.9 32.4 %collective-permute-start = (f32[384,256]{1,0:T(8,128)S(1)}, f32[384,256]{1,0:T(8,128)S(1)}, u32[]{:S(2)}, u32[]{:S(2)}) collective-permute-start(f32[384,256]{1,0:T(8,128)S(1)} %fusion.11), channel_id=1, source_target_pairs={{4,0},{8,4},{12,8},{5,1},{9,5},{13,9},{6,2},{10,6},{14,10},{7,3},{... | collective-permute-start | bytes 1179656 | tf_op jit(solution)/shard_map/ppermute | solution.py:15
  428.8 10.6 %collective-permute-start.1 = (f32[384,256]{1,0:T(8,128)S(1)}, f32[384,256]{1,0:T(8,128)S(1)}, u32[]{:S(2)}, u32[]{:S(2)}) collective-permute-start(f32[384,256]{1,0:T(8,128)S(1)} %fusion.8), channel_id=1, source_target_pairs={{4,0},{8,4},{12,8},{5,1},{9,5},{13,9},{6,2},{10,6},{14,10},{7,3},{... | collective-permute-start | bytes 1179656 | tf_op jit(solution)/shard_map/ppermute | solution.py:15
  440.9 10.6 %collective-permute-start.2 = (f32[384,256]{1,0:T(8,128)S(1)}, f32[384,256]{1,0:T(8,128)S(1)}, u32[]{:S(2)}, u32[]{:S(2)}) collective-permute-start(f32[384,256]{1,0:T(8,128)S(1)} %fusion.5), channel_id=1, source_target_pairs={{4,0},{8,4},{12,8},{5,1},{9,5},{13,9},{6,2},{10,6},{14,10},{7,3},{... | collective-permute-start | bytes 1179656 | tf_op jit(solution)/shard_map/ppermute | solution.py:15
Sparse Core Ops, SparseCore 0:
  10.1 78.6 all-gather.1
  99.7 51.2 reduce-scatter.1
  154.3 238.1 all-reduce.2
where the time goes:
time: 462 us; the launch traced here: 461 us
  waiting for transfers between devices  392 us (85%)
  starting transfers between devices  28.5 us (6%)
  between operations  14 us (3%)
  matrix products  13.1 us (3%)
  other arithmetic  7.44 us (2%)
  local copies, waits for them, and re-layouts  6.32 us (1%)
    psum x1, waiting for transfers between devices, local(): gradient = lax.psum(level_part, 'board')  241 us
    all_gather x1, waiting for transfers between devices, local(): piece = lax.all_gather(reach, 'hand', axis=1, tiled=True)  74.4 us
    reduce_scatter x1, waiting for transfers between devices, local(): lax.psum_scatter(partial_value, 'depth', scatter_dimension=1, tiled=True)  51.4 us
    ppermute x3, starting transfers between devices, passed_along(): return lax.ppermute(array, axis, pairs)  28.4 us
    ppermute x3, waiting for transfers between devices, passed_along(): return lax.ppermute(array, axis, pairs)  24.9 us
  transfers between devices with their start and end apart: 6, of which 6 were waited for; matrix products, arithmetic and copies ran while one was open for 2% of the time, Pallas kernels for 0%

commit v1 on v0

v1 whole, which is shorter than its diff:
```python
import jax
import jax.numpy as jnp
import numpy as np
from jax import lax
from jax.experimental import pallas as pl
from jax.experimental.pallas import tpu as pltpu
from jax.sharding import PartitionSpec as P

CARDS = 52
HANDS = 1326
ACT = 4
NZ = 16
NX = 4
NL = 4
NJ = 8
HX = 384
HP = NX * HX
HJ = HX // NJ
HZ = HJ // NZ
SL = 256
SX = NL * SL
NB = 8
BOUND = float(NB * HX)
SCALE = 32767.0 / BOUND
MESH = pl.DeviceIdType.MESH
NAN = float("nan")


def hand_cards():
    first, second = np.triu_indices(CARDS, 1)
    table = np.full((8, HP), -1.0, np.float32)
    table[0, :HANDS] = first
    table[1, :HANDS] = second
    onehot = np.zeros((HP, 128), np.float32)
    onehot[np.arange(HANDS), first] = 1.0
    onehot[np.arange(HANDS), second] = 1.0
    return table, onehot


def dot_t(a, b):
    return lax.dot_general(a, b, (((1,), (1,)), ((), ())), preferred_element_type=jnp.float32)


def group_reduce(x, op):
    lane = lax.broadcasted_iota(jnp.int32, x.shape, 1)
    near = jnp.where(lane % 2 == 0, pltpu.roll(x, 127, 1), pltpu.roll(x, 1, 1))
    x = op(x, near)
    far = jnp.where(lane % 4 < 2, pltpu.roll(x, 126, 1), pltpu.roll(x, 2, 1))
    return op(x, far)


def group_value(scores, legal):
    parts = []
    for half in range(2):
        cols = slice(half * 128, half * 128 + 128)
        masked = jnp.where(legal[:, cols] > 0.0, scores[:, cols], -jnp.inf)
        top = group_reduce(masked, jnp.maximum)
        total = group_reduce(jnp.exp(masked - top), jnp.add)
        parts.append(top + jnp.log(total))
    return jnp.concatenate(parts, axis=1)


def hand_down(value, owner_t):
    a = value.astype(jnp.bfloat16)
    rest = value - a.astype(jnp.float32)
    b = rest.astype(jnp.bfloat16)
    c = (rest - b.astype(jnp.float32)).astype(jnp.bfloat16)
    return dot_t(a, owner_t) + dot_t(b, owner_t) + dot_t(c, owner_t)


def kernel(
    reach,
    payoff,
    cards,
    rank,
    logits,
    counts,
    parents,
    table,
    onehot,
    policy,
    passed,
    ranks,
    ranks_t,
    out1,
    in1,
    out2,
    in2,
    rows8,
    logit8,
    pay,
    logit_rows,
    logit_tiles,
    out3,
    in3,
    out4,
    in4,
    legal,
    owners,
    send1,
    recv1,
    send2,
    recv2,
    send3,
    recv3,
    send4,
    recv4,
    send_p,
    recv_p,
    send_l,
    recv_l,
):
    board = lax.axis_index("board")
    depth = lax.axis_index("depth")
    x = lax.axis_index("hand")
    z = board // 2
    y_lo = board % 2
    j = y_lo * NL + depth

    def device(to_z, to_j, to_x):
        return (to_z * 2 + to_j // NL, to_j % NL, to_x)

    def copy(src, dst, send, recv, to):
        return pltpu.make_async_remote_copy(
            src_ref=src, dst_ref=dst, send_sem=send, recv_sem=recv, device_id=to, device_id_type=MESH
        )

    barrier = pltpu.get_barrier_semaphore()

    @pl.loop(1, NX * NJ)
    def _(step):
        other = (x * NJ + j + step) % (NX * NJ)
        pl.semaphore_signal(barrier, inc=1, device_id=device(z, other % NJ, other // NJ), device_id_type=MESH)

    @pl.loop(1, NZ)
    def _(step):
        pl.semaphore_signal(barrier, inc=1, device_id=device((z + step) % NZ, j, x), device_id_type=MESH)

    ranks[...] = jnp.full((NB, HP), NAN, jnp.float32)
    ranks[:, :HANDS] = rank[...].astype(jnp.float32)
    first = table[0:1, :]
    second = table[1:2, :]
    hit = first < 0.0
    for card in range(5):
        one = cards[:, card : card + 1].astype(jnp.float32)
        hit = hit | (first == one) | (second == one)
    ranks[...] = jnp.where(hit, NAN, ranks[...])
    ranks_t[...] = ranks[...].T

    own = pl.ds(pl.multiple_of(x * HX, HX), HX)

    def partial(to_x):
        rows = pl.ds(pl.multiple_of(to_x * HX, HX), HX)
        shared = dot_t(onehot[rows, :], onehot[own, :])
        apart = jnp.where(shared > 0.0, 0.0, 1.0)
        minus = -apart
        total = jnp.zeros((HX, SL), jnp.float32)
        for pair in range(NB // 2):
            sides = []
            for b in (2 * pair, 2 * pair + 1):
                mine = ranks_t[rows, b : b + 1]
                theirs = ranks[b : b + 1, own]
                sign = jnp.where(theirs < mine, apart, jnp.where(theirs > mine, minus, 0.0))
                sides.append(sign.astype(jnp.bfloat16))
            total += jnp.dot(
                jnp.concatenate(sides, axis=1),
                reach[2 * HX * pair : 2 * HX * (pair + 1), :],
                preferred_element_type=jnp.float32,
            )
        return jnp.round(total * SCALE).astype(jnp.int32).astype(jnp.int16)

    out1[0] = partial((x + 2) % NX).reshape(NJ, HJ, SL)
    pl.semaphore_wait(barrier, NX * NJ - 1 + NZ - 1)

    me1 = depth * NJ + x * 2 + y_lo

    def send_chunk(i):
        to_x = (x + 2 + i) % NX

        @pl.loop(0, NJ)
        def _(to_j):
            copy(
                out1.at[i, to_j], in1.at[me1], send1.at[i, to_j], recv1.at[me1], device(z, to_j, to_x)
            ).start()

    send_chunk(0)

    for i in (1, 3):
        out1[i] = partial((x + 2 + i) % NX).reshape(NJ, HJ, SL)
        send_chunk(i)
    out1[2] = partial(x).reshape(NJ, HJ, SL)

    @pl.loop(1, NJ)
    def _(step):
        to_j = (j + step) % NJ
        copy(out1.at[2, to_j], in1.at[me1], send1.at[2, to_j], recv1.at[me1], device(z, to_j, x)).start()

    in1[me1] = out1[2, j]

    def depth_peer(step):
        return (depth + step) % NL

    for step in range(1, NL):
        to = y_lo * NL + depth_peer(step)
        copy(
            logits.at[pl.ds(pl.multiple_of(to * HJ, HJ), HJ)],
            logit_rows.at[depth],
            send_l.at[step],
            recv_l.at[depth],
            device(z, to, x),
        ).start()
    logit_rows[depth] = logits[pl.ds(pl.multiple_of(j * HJ, HJ), HJ), :]
    pay[depth] = payoff[...]
    across = depth_peer(2)
    beside = depth + 1 - 2 * (depth % 2)
    opposite = across + 1 - 2 * (across % 2)
    pay_across = copy(payoff, pay.at[depth], send_p.at[0], recv_p.at[depth], device(z, y_lo * NL + across, x))
    pay_across.start()
    pay_beside = copy(payoff, pay.at[depth], send_p.at[1], recv_p.at[depth], device(z, y_lo * NL + beside, x))
    pay_beside.start()

    spread = (
        lax.broadcasted_iota(jnp.int32, (SL // ACT, SL), 0)
        == lax.broadcasted_iota(jnp.int32, (SL // ACT, SL), 1) // ACT
    ).astype(jnp.bfloat16)
    lane = lax.broadcasted_iota(jnp.int32, (NL, SL), 1) % ACT
    counts_wide = jnp.dot(
        counts[...].astype(jnp.float32).astype(jnp.bfloat16), spread, preferred_element_type=jnp.float32
    )
    parents_wide = jnp.dot(
        parents[...].astype(jnp.float32).astype(jnp.bfloat16), spread, preferred_element_type=jnp.float32
    )
    legal[...] = jnp.where(lane.astype(jnp.float32) < counts_wide, 1.0, 0.0)
    parents_wide = jnp.where(lane == 0, parents_wide, -1.0)
    seq = lax.broadcasted_iota(jnp.int32, (SL, SL), 0).astype(jnp.float32)
    for level in range(NL):
        owners[level] = jnp.where(seq == parents_wide[level : level + 1, :], 1.0, 0.0).astype(jnp.bfloat16)

    @pl.loop(1, NX * NJ)
    def _(step):
        slot = (me1 + step) % (NX * NJ)
        copy(in1.at[slot], in1.at[slot], send1.at[0, 0], recv1.at[slot], device(z, (j + 1) % NJ, x)).wait_recv()

    for block in range(NL):
        total = in1[block * NJ].astype(jnp.int32)
        for source in range(1, NJ):
            total += in1[block * NJ + source].astype(jnp.int32)
        total = total.astype(jnp.float32)
        out2[:, 2 * block, :] = total[:, :128]
        out2[:, 2 * block + 1, :] = total[:, 128:]

    @pl.loop(1, NZ)
    def _(step):
        to_z = (z + step) % NZ
        copy(
            out2.at[pl.ds(to_z * HZ, HZ)], in2.at[z], send2.at[step], recv2.at[z], device(to_z, j, x)
        ).start()

    in2[z] = out2[pl.ds(z * HZ, HZ)]

    copy(payoff, pay.at[across], send_p.at[0], recv_p.at[across], device(z, (j + 1) % NJ, x)).wait_recv()
    pay_on = copy(
        pay.at[across], pay.at[across], send_p.at[2], recv_p.at[across], device(z, y_lo * NL + beside, x)
    )
    pay_on.start()
    copy(payoff, pay.at[beside], send_p.at[0], recv_p.at[beside], device(z, (j + 1) % NJ, x)).wait_recv()
    copy(payoff, pay.at[opposite], send_p.at[0], recv_p.at[opposite], device(z, (j + 1) % NJ, x)).wait_recv()

    rows8[...] = jnp.zeros((8, SX), jnp.float32)
    logit8[...] = jnp.zeros((8, SX), jnp.float32)
    for step in range(1, NL):
        slot = depth_peer(step)
        copy(
            logit_rows.at[slot], logit_rows.at[slot], send_l.at[0], recv_l.at[slot], device(z, (j + 1) % NJ, x)
        ).wait_recv()
    for group in range(8):
        logit_tiles[:, group, :] = logit_rows[group // 2, :, (group % 2) * 128 : (group % 2) * 128 + 128]
    for group in range(8):
        logit8[0:HZ, group * 128 : (group + 1) * 128] = logit_tiles[pl.ds(z * HZ, HZ), group, :]

    @pl.loop(1, NZ)
    def _(step):
        slot = (z + step) % NZ
        copy(in2.at[slot], in2.at[slot], send2.at[0], recv2.at[slot], device(slot, j, x)).wait_recv()

    total = in2[0]
    for source in range(1, NZ):
        total += in2[source]
    in2[0] = total
    for group in range(8):
        rows8[0:HZ, group * 128 : (group + 1) * 128] = in2[0, :, group, :]
    counter = rows8[...]
    high = counter.astype(jnp.bfloat16).astype(jnp.float32)
    both = jnp.concatenate([high, counter - high], axis=0).astype(jnp.bfloat16)
    gradient = jnp.dot(both[:, :SL], pay[0], preferred_element_type=jnp.float32)
    for block in range(1, NL):
        gradient += jnp.dot(
            both[:, block * SL : (block + 1) * SL], pay[block], preferred_element_type=jnp.float32
        )
    gradient = (gradient[:8] + gradient[8:]) * (1.0 / SCALE)

    incoming = jnp.zeros((8, SL), jnp.float32)
    for level in range(NL - 1, -1, -1):
        cols = slice(level * SL, (level + 1) * SL)
        shift = gradient[:, cols] + incoming
        out3[:, 2 * level, :] = shift[:HZ, :128]
        out3[:, 2 * level + 1, :] = shift[:HZ, 128:]
        if level:
            value = group_value(logit8[:, cols] + shift, legal[level : level + 1, :])
            incoming = hand_down(value, owners[level])

    @pl.loop(1, NZ)
    def _(step):
        to_z = (z + step) % NZ
        copy(out3, in3.at[z], send3.at[step], recv3.at[z], device(to_z, j, x)).start()

    in3[z] = out3[...]

    @pl.loop(1, NZ)
    def _(step):
        slot = (z + step) % NZ
        copy(in3.at[slot], in3.at[slot], send3.at[0], recv3.at[slot], device(slot, j, x)).wait_recv()

    shifts = in3[...].reshape(HJ, 8, 128)
    for level in range(NL):
        out4[level, :, :128] = shifts[:, 2 * level, :]
        out4[level, :, 128:] = shifts[:, 2 * level + 1, :]

    @pl.loop(1, NJ)
    def _(step):
        to_j = (j + step) % NJ
        copy(out4.at[to_j % NL], in4.at[j], send4.at[step], recv4.at[j], device(z, to_j, x)).start()

    in4[j] = out4[depth]

    @pl.loop(1, NJ)
    def _(step):
        slot = (j + step) % NJ
        copy(in4.at[slot], in4.at[slot], send4.at[0], recv4.at[slot], device(z, slot, x)).wait_recv()

    scores = logits[...] + in4[...].reshape(HX, SL)
    can = legal[pl.ds(depth, 1), :]
    value = group_value(scores, can)
    policy[...] = jnp.where(can > 0.0, scores - value, 0.0)
    passed[...] = hand_down(value, owners[depth])

    for i in (0, 1, 3):

        @pl.loop(0, NJ)
        def _(to_j):
            copy(
                out1.at[i, to_j], in1.at[me1], send1.at[i, to_j], recv1.at[me1], device(z, (j + 1) % NJ, x)
            ).wait_send()

    @pl.loop(1, NJ)
    def _(step):
        to_j = (j + step) % NJ
        copy(out1.at[2, to_j], in1.at[me1], send1.at[2, to_j], recv1.at[me1], device(z, to_j, x)).wait_send()
        copy(out4.at[to_j % NL], in4.at[j], send4.at[step], recv4.at[j], device(z, to_j, x)).wait_send()

    @pl.loop(1, NZ)
    def _(step):
        to_z = (z + step) % NZ
        copy(
            out2.at[pl.ds(to_z * HZ, HZ)], in2.at[z], send2.at[step], recv2.at[z], device(to_z, j, x)
        ).wait_send()
        copy(out3, in3.at[z], send3.at[step], recv3.at[z], device(to_z, j, x)).wait_send()

    for step in range(1, NL):
        to = y_lo * NL + depth_peer(step)
        copy(
            logits.at[pl.ds(pl.multiple_of(to * HJ, HJ), HJ)],
            logit_rows.at[depth],
            send_l.at[step],
            recv_l.at[depth],
            device(z, to, x),
        ).wait_send()
    pay_across.wait_send()
    pay_beside.wait_send()
    pay_on.wait_send()


def local(reach, payoff, board_cards, hand_rank, logits, action_counts, parent_seq):
    table, onehot = hand_cards()
    vmem = pl.BlockSpec(memory_space=pltpu.VMEM)
    dma = pltpu.SemaphoreType.DMA
    f32, bf16, i16 = jnp.float32, jnp.bfloat16, jnp.int16
    return pl.pallas_call(
        kernel,
        name="prox",
        out_shape=(jax.ShapeDtypeStruct((HX, SL), f32), jax.ShapeDtypeStruct((HX, SL), f32)),
        in_specs=[vmem] * 9,
        out_specs=(vmem, vmem),
        scratch_shapes=[
            pltpu.VMEM((NB, HP), f32),
            pltpu.VMEM((HP, NB), f32),
            pltpu.VMEM((NX, NJ, HJ, SL), i16),
            pltpu.VMEM((NL * NJ, HJ, SL), i16),
            pltpu.VMEM((HJ, 8, 128), f32),
            pltpu.VMEM((NZ, HZ, 8, 128), f32),
            pltpu.VMEM((8, SX), f32),
            pltpu.VMEM((8, SX), f32),
            pltpu.VMEM((NL, SL, SX), bf16),
            pltpu.VMEM((NL, HJ, SL), f32),
            pltpu.VMEM((HJ, 8, 128), f32),
            pltpu.VMEM((HZ, 8, 128), f32),
            pltpu.VMEM((NZ, HZ, 8, 128), f32),
            pltpu.VMEM((NL, HJ, SL), f32),
            pltpu.VMEM((NJ, HJ, SL), f32),
            pltpu.VMEM((NL, SL), f32),
            pltpu.VMEM((NL, SL, SL), bf16),
            dma((NX, NJ)),
            dma((NL * NJ,)),
            dma((NZ,)),
            dma((NZ,)),
            dma((NZ,)),
            dma((NZ,)),
            dma((NJ,)),
            dma((NJ,)),
            dma((3,)),
            dma((NL,)),
            dma((NL,)),
            dma((NL,)),
        ],
        compiler_params=pltpu.CompilerParams(
            collective_id=0, has_side_effects=True, vmem_limit_bytes=48 * 1024 * 1024
        ),
    )(
        reach.reshape(NB * HX, SL),
        payoff,
        board_cards,
        hand_rank,
        logits,
        action_counts,
        parent_seq,
        jnp.asarray(table),
        jnp.asarray(onehot, jnp.bfloat16),
    )


def solution(mesh):
    return jax.shard_map(
        local,
        mesh=mesh,
        in_specs=(
            P("board", "hand", "depth"),
            P("depth", None),
            P("board", None),
            P("board", None),
            P("hand", "depth"),
            P(),
            P(),
        ),
        out_specs=(P("hand", "depth"), P("hand", "depth")),
        check_vma=False,
    )
```

time: 462 us -> 83 us (0.18)
  waiting for transfers between devices: 392 us -> 0 us
  Pallas kernels: 0 us -> 72.3 us
  starting transfers between devices: 28.5 us -> 0 us
  between operations: 14 us -> 0.66 us
  matrix products: 13.1 us -> 0 us
  other arithmetic: 7.44 us -> 0 us
    psum x1 -> x0, waiting for transfers between devices: 241 us -> none  [local(): gradient = lax.psum(level_part, 'board')]
    all_gather x1 -> x0, waiting for transfers between devices: 74.4 us -> none  [local(): piece = lax.all_gather(reach, 'hand', axis=1, tiled=True)]
    pallas_call x0 -> x1, Pallas kernels: none -> 72.3 us  [local(): pl.pallas_call(kernel, name='prox', out_shape=(jax.ShapeDtypeStruct((HX,...]
    reduce_scatter x1 -> x0, waiting for transfers between devices: 51.4 us -> none  [local(): lax.psum_scatter(partial_value, 'depth', scatter_dimension=1, tiled=True)]
    ppermute x3 -> x0, starting transfers between devices: 28.4 us -> none  [passed_along(): return lax.ppermute(array, axis, pairs)]
    ppermute x3 -> x0, waiting for transfers between devices: 24.9 us -> none  [passed_along(): return lax.ppermute(array, axis, pairs)]
    dot_general x6 -> x0, matrix products: 13.1 us -> none  [the longest x1 8.88 us: local(): jnp.einsum('bhk,bks->bhs', block, piece, preferred_element_type=jnp.float32)]
    unnamed x5 -> x20, local copies, waits for them, and re-layouts: 0.78 us -> 9.56 us
  transfers between devices with their start and end apart: 6 -> 0, of which waited for: 6 -> 0; matrix products, arithmetic and copies ran while one was open for 2% -> 0% of each run, Pallas kernels for 0% -> 0%
where the time goes in v1:
time: 83 us; the launch traced here: 82.5 us
  Pallas kernels  72.3 us (87%)
  local copies, waits for them, and re-layouts  9.56 us (12%)
    pallas_call x1, Pallas kernels, local(): pl.pallas_call(kernel, name='prox', out_shape=(jax.ShapeDtypeStruct((HX,...  72.3 us
    unnamed x20, local copies, waits for them, and re-layouts  9.56 us

profile of v1, /device:TPU:1, one launch (start us, length us, event | category | flops | bytes accessed | tf_op | source)
XLA Modules:
  0.0 82.5 jit_solution(15461150206327896404)
XLA Ops:
  0.6 0.0 copy-start
  0.6 1.4 %copy-done = bf16[8,384,256]{2,1,0:T(8,128)(2,1)S(1)} copy-done((bf16[8,384,256]{2,1,0:T(8,128)(2,1)S(1)}, bf16[8,384,256]{2,1,0:T(8,128)(2,1)}, u32[]{:S(2)}) %copy-start) | copy-done | bytes 1572888
  2.0 0.0 copy-start.1
  2.0 1.0 %copy-done.1 = bf16[256,1024]{1,0:T(8,128)(2,1)S(1)} copy-done((bf16[256,1024]{1,0:T(8,128)(2,1)S(1)}, bf16[256,1024]{1,0:T(8,128)(2,1)}, u32[]{:S(2)}) %copy-start.1) | copy-done | bytes 524312
  3.1 0.0 copy-start.2
  3.1 1.0 %copy-done.2 = f32[384,256]{1,0:T(8,128)S(1)} copy-done((f32[384,256]{1,0:T(8,128)S(1)}, f32[384,256]{1,0:T(8,128)}, u32[]{:S(2)}) %copy-start.2) | copy-done | bytes 393240
  4.1 0.0 copy-start.3
  4.1 1.0 %copy-done.3 = bf16[1536,128]{1,0:T(8,128)(2,1)S(1)} copy-done((bf16[1536,128]{1,0:T(8,128)(2,1)S(1)}, bf16[1536,128]{1,0:T(8,128)(2,1)}, u32[]{:S(2)}) %copy-start.3) | copy-done | bytes 393240
  5.1 0.0 copy-start.4
  5.1 0.8 copy-done.4
  5.9 0.0 copy-start.5
  5.9 0.8 copy-done.5
  6.7 0.0 copy-start.6
  6.7 0.7 copy-done.6
  7.4 0.0 copy-start.7
  7.4 0.7 copy-done.7
  8.0 0.0 copy-start.8
  8.0 0.7 copy-done.8
  8.7 72.3 %prox.1 = (f32[384,256]{1,0:T(8,128)S(1)}, f32[384,256]{1,0:T(8,128)S(1)}) custom-call(bf16[3072,256]{1,0:T(8,128)(2,1)S(1)} %bitcast.1, bf16[256,1024]{1,0:T(8,128)(2,1)S(1)} %copy-done.1, s32[8,5]{1,0:T(8,128)S(1)} %copy-done.6, s32[8,1326]{1,0:T(8,128)S(1)} %copy-done.5, f32[384,256]{1,0:T(8,128)S(1)} %copy-done.2, s32[4,64]{1,0:T(4,128)S(1)} %copy-done.7, ...), custom_call_target="tpu_custom_call" | custom-call | tf_op jit(solution)/shard_map/prox/pallas_call | solution.py:388
  81.0 0.7 copy.13
  81.8 0.7 copy.14
Async XLA Ops:
  0.6 1.4 %copy-start = (bf16[8,384,256]{2,1,0:T(8,128)(2,1)S(1)}, bf16[8,384,256]{2,1,0:T(8,128)(2,1)}, u32[]{:S(2)}) copy-start(bf16[8,384,256]{2,1,0:T(8,128)(2,1)} %param.9) | copy-start | bytes 4718596
  2.0 1.0 %copy-start.1 = (bf16[256,1024]{1,0:T(8,128)(2,1)S(1)}, bf16[256,1024]{1,0:T(8,128)(2,1)}, u32[]{:S(2)}) copy-start(bf16[256,1024]{1,0:T(8,128)(2,1)} %payoff.1) | copy-start | bytes 1572868
  3.1 1.0 %copy-start.2 = (f32[384,256]{1,0:T(8,128)S(1)}, f32[384,256]{1,0:T(8,128)}, u32[]{:S(2)}) copy-start(f32[384,256]{1,0:T(8,128)} %logits.1) | copy-start | bytes 1179652
  4.1 1.0 %copy-start.3 = (bf16[1536,128]{1,0:T(8,128)(2,1)S(1)}, bf16[1536,128]{1,0:T(8,128)(2,1)}, u32[]{:S(2)}) copy-start(bf16[1536,128]{1,0:T(8,128)(2,1)} %constant.5.clone.onehot) | copy-start | bytes 1179652
  5.1 0.8 copy-start.4
  5.9 0.8 copy-start.5
  6.7 0.7 copy-start.6
  7.4 0.7 copy-start.7
  8.0 0.7 copy-start.8

commit v2 on v1

--- a/solution.py
+++ b/solution.py
@@ -23,6 +23,13 @@
 BOUND = float(NB * HX)
 SCALE = 32767.0 / BOUND
 MESH = pl.DeviceIdType.MESH
+NEAR = (1, -1, 2, -2)
+UP = (3, 4, 6, 7, 8)
+DOWN = (-3, -4, -6, -7)
+HUB = 5
+PEERS = (1, -1, 2, -2, 3, -3, 5, -5)
+PLACES = (0, 1, -1, 2, -2, 5, -5, 3, 4, 6, 7, 8, -3, -4, -6, -7)
+EARLY = 7
 NAN = float("nan")
 
 
@@ -69,8 +76,18 @@
 
 
 def kernel(
+    reach_hbm,
+    payoff,
+    cards_hbm,
+    rank_hbm,
+    logits_hbm,
+    counts_hbm,
+    parents_hbm,
+    table_hbm,
+    onehot_hbm,
+    policy,
+    passed,
     reach,
-    payoff,
     cards,
     rank,
     logits,
@@ -78,8 +95,7 @@
     parents,
     table,
     onehot,
-    policy,
-    passed,
+    load,
     ranks,
     ranks_t,
     out1,
@@ -91,10 +107,10 @@
     pay,
     logit_rows,
     logit_tiles,
-    out3,
+    mid2,
     in3,
-    out4,
     in4,
+    shifts,
     legal,
     owners,
     send1,
@@ -120,11 +136,33 @@
     def device(to_z, to_j, to_x):
         return (to_z * 2 + to_j // NL, to_j % NL, to_x)
 
+    def along(dz):
+        return (z + dz + NZ) % NZ
+
     def copy(src, dst, send, recv, to):
         return pltpu.make_async_remote_copy(
             src_ref=src, dst_ref=dst, send_sem=send, recv_sem=recv, device_id=to, device_id_type=MESH
         )
 
+    loads = [
+        pltpu.make_async_copy(src, dst, load.at[i])
+        for i, (src, dst) in enumerate(
+            [
+                (rank_hbm, rank),
+                (cards_hbm, cards),
+                (table_hbm, table),
+                (onehot_hbm, onehot),
+                (reach_hbm, reach),
+                (payoff, pay.at[depth]),
+                (logits_hbm, logits),
+                (counts_hbm, counts),
+                (parents_hbm, parents),
+            ]
+        )
+    ]
+    for one in loads:
+        one.start()
+
     barrier = pltpu.get_barrier_semaphore()
 
     @pl.loop(1, NX * NJ)
@@ -132,9 +170,11 @@
         other = (x * NJ + j + step) % (NX * NJ)
         pl.semaphore_signal(barrier, inc=1, device_id=device(z, other % NJ, other // NJ), device_id_type=MESH)
 
-    @pl.loop(1, NZ)
-    def _(step):
-        pl.semaphore_signal(barrier, inc=1, device_id=device((z + step) % NZ, j, x), device_id_type=MESH)
+    for dz in PEERS:
+        pl.semaphore_signal(barrier, inc=1, device_id=device(along(dz), j, x), device_id_type=MESH)
+
+    for one in loads[:3]:
+        one.wait()
 
     ranks[...] = jnp.full((NB, HP), NAN, jnp.float32)
     ranks[:, :HANDS] = rank[...].astype(jnp.float32)
@@ -148,6 +188,9 @@
     ranks_t[...] = ranks[...].T
 
     own = pl.ds(pl.multiple_of(x * HX, HX), HX)
+
+    loads[3].wait()
+    loads[4].wait()
 
     def partial(to_x):
         rows = pl.ds(pl.multiple_of(to_x * HX, HX), HX)
@@ -169,33 +212,34 @@
             )
         return jnp.round(total * SCALE).astype(jnp.int32).astype(jnp.int16)
 
-    out1[0] = partial((x + 2) % NX).reshape(NJ, HJ, SL)
-    pl.semaphore_wait(barrier, NX * NJ - 1 + NZ - 1)
+    @pl.loop(0, NX)
+    def _(i):
+        out1[i] = partial(i).reshape(NJ, HJ, SL)
+
+    pl.semaphore_wait(barrier, NX * NJ - 1 + len(PEERS))
 
     me1 = depth * NJ + x * 2 + y_lo
 
-    def send_chunk(i):
-        to_x = (x + 2 + i) % NX
-
-        @pl.loop(0, NJ)
-        def _(to_j):
-            copy(
-                out1.at[i, to_j], in1.at[me1], send1.at[i, to_j], recv1.at[me1], device(z, to_j, to_x)
-            ).start()
-
-    send_chunk(0)
-
-    for i in (1, 3):
-        out1[i] = partial((x + 2 + i) % NX).reshape(NJ, HJ, SL)
-        send_chunk(i)
-    out1[2] = partial(x).reshape(NJ, HJ, SL)
-
-    @pl.loop(1, NJ)
-    def _(step):
-        to_j = (j + step) % NJ
-        copy(out1.at[2, to_j], in1.at[me1], send1.at[2, to_j], recv1.at[me1], device(z, to_j, x)).start()
-
-    in1[me1] = out1[2, j]
+    def row_copy(step):
+        turn = step // NX
+        to_y_lo = (y_lo + (turn // 2 + 1) // 2) % 2
+        to_y_hi = (depth // 2 + 1 - turn // 4) % 2
+        to_core = (depth + 1 - turn % 2) % 2
+        to_j = to_y_lo * NL + to_y_hi * 2 + to_core
+        hop = step % NX
+        to_x = (x + 2 + hop + hop * (hop - 1) // 2) % NX
+        return copy(
+            out1.at[to_x, to_j], in1.at[me1], send1.at[step], recv1.at[me1], device(z, to_j, to_x)
+        )
+
+    @pl.loop(0, NX * NJ - 1)
+    def _(step):
+        row_copy(step).start()
+
+    in1[me1] = out1[x, j]
+
+    for one in loads[5:]:
+        one.wait()
 
     def depth_peer(step):
         return (depth + step) % NL
@@ -210,13 +254,12 @@
             device(z, to, x),
         ).start()
     logit_rows[depth] = logits[pl.ds(pl.multiple_of(j * HJ, HJ), HJ), :]
-    pay[depth] = payoff[...]
     across = depth_peer(2)
     beside = depth + 1 - 2 * (depth % 2)
     opposite = across + 1 - 2 * (across % 2)
-    pay_across = copy(payoff, pay.at[depth], send_p.at[0], recv_p.at[depth], device(z, y_lo * NL + across, x))
+    pay_across = copy(pay.at[depth], pay.at[depth], send_p.at[0], recv_p.at[depth], device(z, y_lo * NL + across, x))
     pay_across.start()
-    pay_beside = copy(payoff, pay.at[depth], send_p.at[1], recv_p.at[depth], device(z, y_lo * NL + beside, x))
+    pay_beside = copy(pay.at[depth], pay.at[depth], send_p.at[1], recv_p.at[depth], device(z, y_lo * NL + beside, x))
     pay_beside.start()
 
     spread = (
@@ -239,7 +282,7 @@
     @pl.loop(1, NX * NJ)
     def _(step):
         slot = (me1 + step) % (NX * NJ)
-        copy(in1.at[slot], in1.at[slot], send1.at[0, 0], recv1.at[slot], device(z, (j + 1) % NJ, x)).wait_recv()
+        copy(in1.at[slot], in1.at[slot], send1.at[0], recv1.at[slot], device(z, (j + 1) % NJ, x)).wait_recv()
 
     for block in range(NL):
         total = in1[block * NJ].astype(jnp.int32)
@@ -249,22 +292,45 @@
         out2[:, 2 * block, :] = total[:, :128]
         out2[:, 2 * block + 1, :] = total[:, 128:]
 
-    @pl.loop(1, NZ)
-    def _(step):
-        to_z = (z + step) % NZ
-        copy(
-            out2.at[pl.ds(to_z * HZ, HZ)], in2.at[z], send2.at[step], recv2.at[z], device(to_z, j, x)
-        ).start()
-
-    in2[z] = out2[pl.ds(z * HZ, HZ)]
-
-    copy(payoff, pay.at[across], send_p.at[0], recv_p.at[across], device(z, (j + 1) % NJ, x)).wait_recv()
+    def block2(dz):
+        return out2.at[pl.ds(along(dz) * HZ, HZ)]
+
+    sums = []
+    for i, k in enumerate(UP):
+        sums.append((block2(-k), i, HUB - k))
+    for i, k in enumerate(DOWN):
+        sums.append((block2(-k), len(UP) + i, -HUB - k))
+    for i, dz in enumerate(NEAR):
+        sums.append((block2(dz), len(UP) + len(DOWN) + i, dz))
+
+    def copy2(src, slot, dz):
+        return copy(src, in2.at[slot], send2.at[slot], recv2.at[slot], device(along(dz), j, x))
+
+    for src, slot, dz in sums:
+        copy2(src, slot, dz).start()
+
+    def wait2(slots):
+        total = None
+        for slot in slots:
+            copy2(in2.at[slot], slot, 1).wait_recv()
+        for slot in slots:
+            total = in2[slot] if total is None else total + in2[slot]
+        return total
+
+    n_up, n_far = len(UP), len(UP) + len(DOWN)
+    n_all = n_far + len(NEAR)
+    mid2[0] = wait2(range(n_up)) + out2[pl.ds(along(-HUB) * HZ, HZ)]
+    copy2(mid2.at[0], n_all, -HUB).start()
+    mid2[1] = wait2(range(n_up, n_far)) + out2[pl.ds(along(HUB) * HZ, HZ)]
+    copy2(mid2.at[1], n_all + 1, HUB).start()
+
+    copy(pay.at[depth], pay.at[across], send_p.at[0], recv_p.at[across], device(z, (j + 1) % NJ, x)).wait_recv()
     pay_on = copy(
         pay.at[across], pay.at[across], send_p.at[2], recv_p.at[across], device(z, y_lo * NL + beside, x)
     )
     pay_on.start()
-    copy(payoff, pay.at[beside], send_p.at[0], recv_p.at[beside], device(z, (j + 1) % NJ, x)).wait_recv()
-    copy(payoff, pay.at[opposite], send_p.at[0], recv_p.at[opposite], device(z, (j + 1) % NJ, x)).wait_recv()
+    copy(pay.at[depth], pay.at[beside], send_p.at[0], recv_p.at[beside], device(z, (j + 1) % NJ, x)).wait_recv()
+    copy(pay.at[depth], pay.at[opposite], send_p.at[0], recv_p.at[opposite], device(z, (j + 1) % NJ, x)).wait_recv()
 
     rows8[...] = jnp.zeros((8, SX), jnp.float32)
     logit8[...] = jnp.zeros((8, SX), jnp.float32)
@@ -278,17 +344,9 @@
     for group in range(8):
         logit8[0:HZ, group * 128 : (group + 1) * 128] = logit_tiles[pl.ds(z * HZ, HZ), group, :]
 
-    @pl.loop(1, NZ)
-    def _(step):
-        slot = (z + step) % NZ
-        copy(in2.at[slot], in2.at[slot], send2.at[0], recv2.at[slot], device(slot, j, x)).wait_recv()
-
-    total = in2[0]
-    for source in range(1, NZ):
-        total += in2[source]
-    in2[0] = total
+    mid2[2] = wait2(range(n_far, n_all + 2)) + out2[pl.ds(z * HZ, HZ)]
     for group in range(8):
-        rows8[0:HZ, group * 128 : (group + 1) * 128] = in2[0, :, group, :]
+        rows8[0:HZ, group * 128 : (group + 1) * 128] = mid2[2, :, group, :]
     counter = rows8[...]
     high = counter.astype(jnp.bfloat16).astype(jnp.float32)
     both = jnp.concatenate([high, counter - high], axis=0).astype(jnp.bfloat16)
@@ -303,68 +361,101 @@
     for level in range(NL - 1, -1, -1):
         cols = slice(level * SL, (level + 1) * SL)
         shift = gradient[:, cols] + incoming
-        out3[:, 2 * level, :] = shift[:HZ, :128]
-        out3[:, 2 * level + 1, :] = shift[:HZ, 128:]
+        in3[0, level, :, 0, :] = shift[:HZ, :128]
+        in3[0, level, :, 1, :] = shift[:HZ, 128:]
         if level:
             value = group_value(logit8[:, cols] + shift, legal[level : level + 1, :])
             incoming = hand_down(value, owners[level])
 
-    @pl.loop(1, NZ)
-    def _(step):
-        to_z = (z + step) % NZ
-        copy(out3, in3.at[z], send3.at[step], recv3.at[z], device(to_z, j, x)).start()
-
-    in3[z] = out3[...]
-
-    @pl.loop(1, NZ)
-    def _(step):
-        slot = (z + step) % NZ
-        copy(in3.at[slot], in3.at[slot], send3.at[0], recv3.at[slot], device(slot, j, x)).wait_recv()
-
-    shifts = in3[...].reshape(HJ, 8, 128)
-    for level in range(NL):
-        out4[level, :, :128] = shifts[:, 2 * level, :]
-        out4[level, :, 128:] = shifts[:, 2 * level + 1, :]
+    def copy3(source, dz):
+        slot = PLACES.index(source)
+        there = PLACES.index((source - dz + 7) % NZ - 7)
+        return copy(in3.at[slot], in3.at[there], send3.at[there], recv3.at[there], device(along(dz), j, x))
+
+    def wait3(source):
+        slot = PLACES.index(source)
+        copy(in3.at[slot], in3.at[slot], send3.at[slot], recv3.at[slot], device(along(1), j, x)).wait_recv()
+
+    straight = [copy3(0, dz) for dz in (HUB, -HUB) + NEAR]
+    onward = [copy3(-HUB, k - HUB) for k in UP]
+    onward_down = [copy3(HUB, k + HUB) for k in DOWN]
+    for one in straight:
+        one.start()
+    wait3(-HUB)
+    for one in onward:
+        one.start()
+    wait3(HUB)
+    for one in onward_down:
+        one.start()
+
+    def copy4(step, part):
+        slots = pl.ds(0, EARLY) if part == 0 else pl.ds(EARLY, NZ - EARLY)
+        to_j = (j + step) % NJ
+        return copy(
+            in3.at[slots, to_j % NL],
+            in4.at[j, slots],
+            send4.at[part, step],
+            recv4.at[part, j],
+            device(z, to_j, x),
+        )
+
+    for source in NEAR:
+        wait3(source)
 
     @pl.loop(1, NJ)
     def _(step):
-        to_j = (j + step) % NJ
-        copy(out4.at[to_j % NL], in4.at[j], send4.at[step], recv4.at[j], device(z, to_j, x)).start()
-
-    in4[j] = out4[depth]
+        copy4(step, 0).start()
+
+    for source in PLACES[EARLY:]:
+        wait3(source)
 
     @pl.loop(1, NJ)
     def _(step):
-        slot = (j + step) % NJ
-        copy(in4.at[slot], in4.at[slot], send4.at[0], recv4.at[slot], device(z, slot, x)).wait_recv()
-
-    scores = logits[...] + in4[...].reshape(HX, SL)
+        copy4(step, 1).start()
+
+    def place(from_j, block, slots):
+        for slot in slots:
+            rows = pl.ds((from_j * NZ + along(PLACES[slot])) * HZ, HZ)
+            shifts[rows] = block(slot)
+
+    place(j, lambda slot: in3[slot, depth], range(NZ))
+
+    for part, slots in enumerate((range(EARLY), range(EARLY, NZ))):
+        whole = pl.ds(slots[0], len(slots))
+
+        @pl.loop(1, NJ)
+        def _(step):
+            slot = (j + step) % NJ
+            copy(
+                in4.at[slot, whole],
+                in4.at[slot, whole],
+                send4.at[part, 0],
+                recv4.at[part, slot],
+                device(z, slot, x),
+            ).wait_recv()
+            place(slot, lambda one: in4[slot, one], slots)
+
+    scores = logits[...] + jnp.concatenate([shifts[:, 0, :], shifts[:, 1, :]], axis=1)
     can = legal[pl.ds(depth, 1), :]
     value = group_value(scores, can)
     policy[...] = jnp.where(can > 0.0, scores - value, 0.0)
     passed[...] = hand_down(value, owners[depth])
 
-    for i in (0, 1, 3):
-
-        @pl.loop(0, NJ)
-        def _(to_j):
-            copy(
-                out1.at[i, to_j], in1.at[me1], send1.at[i, to_j], recv1.at[me1], device(z, (j + 1) % NJ, x)
-            ).wait_send()
+    @pl.loop(0, NX * NJ - 1)
+    def _(step):
+        row_copy(step).wait_send()
+
+    for src, slot, dz in sums:
+        copy2(src, slot, dz).wait_send()
+    copy2(mid2.at[0], n_all, -HUB).wait_send()
+    copy2(mid2.at[1], n_all + 1, HUB).wait_send()
+    for one in straight + onward + onward_down:
+        one.wait_send()
 
     @pl.loop(1, NJ)
     def _(step):
-        to_j = (j + step) % NJ
-        copy(out1.at[2, to_j], in1.at[me1], send1.at[2, to_j], recv1.at[me1], device(z, to_j, x)).wait_send()
-        copy(out4.at[to_j % NL], in4.at[j], send4.at[step], recv4.at[j], device(z, to_j, x)).wait_send()
-
-    @pl.loop(1, NZ)
-    def _(step):
-        to_z = (z + step) % NZ
-        copy(
-            out2.at[pl.ds(to_z * HZ, HZ)], in2.at[z], send2.at[step], recv2.at[z], device(to_z, j, x)
-        ).wait_send()
-        copy(out3, in3.at[z], send3.at[step], recv3.at[z], device(to_z, j, x)).wait_send()
+        copy4(step, 0).wait_send()
+        copy4(step, 1).wait_send()
 
     for step in range(1, NL):
         to = y_lo * NL + depth_peer(step)
@@ -389,9 +480,18 @@
         kernel,
         name="prox",
         out_shape=(jax.ShapeDtypeStruct((HX, SL), f32), jax.ShapeDtypeStruct((HX, SL), f32)),
-        in_specs=[vmem] * 9,
+        in_specs=[pl.BlockSpec(memory_space=pl.ANY)] * 9,
         out_specs=(vmem, vmem),
         scratch_shapes=[
+            pltpu.VMEM((NB * HX, SL), bf16),
+            pltpu.VMEM((NB, 5), jnp.int32),
+            pltpu.VMEM((NB, HANDS), jnp.int32),
+            pltpu.VMEM((HX, SL), f32),
+            pltpu.VMEM((NL, SL // ACT), jnp.int32),
+            pltpu.VMEM((NL, SL // ACT), jnp.int32),
+            pltpu.VMEM((8, HP), f32),
+            pltpu.VMEM((HP, 128), bf16),
+            dma((9,)),
             pltpu.VMEM((NB, HP), f32),
             pltpu.VMEM((HP, NB), f32),
             pltpu.VMEM((NX, NJ, HJ, SL), i16),
@@ -403,27 +503,27 @@
             pltpu.VMEM((NL, SL, SX), bf16),
             pltpu.VMEM((NL, HJ, SL), f32),
             pltpu.VMEM((HJ, 8, 128), f32),
-            pltpu.VMEM((HZ, 8, 128), f32),
-            pltpu.VMEM((NZ, HZ, 8, 128), f32),
-            pltpu.VMEM((NL, HJ, SL), f32),
-            pltpu.VMEM((NJ, HJ, SL), f32),
+            pltpu.VMEM((3, HZ, 8, 128), f32),
+            pltpu.VMEM((NZ, NL, HZ, 2, 128), f32),
+            pltpu.VMEM((NJ, NZ, HZ, 2, 128), f32),
+            pltpu.VMEM((HX, 2, 128), f32),
             pltpu.VMEM((NL, SL), f32),
             pltpu.VMEM((NL, SL, SL), bf16),
-            dma((NX, NJ)),
+            dma((NX * NJ,)),
             dma((NL * NJ,)),
             dma((NZ,)),
             dma((NZ,)),
             dma((NZ,)),
             dma((NZ,)),
-            dma((NJ,)),
-            dma((NJ,)),
+            dma((2, NJ)),
+            dma((2, NJ)),
             dma((3,)),
             dma((NL,)),
             dma((NL,)),
             dma((NL,)),
         ],
         compiler_params=pltpu.CompilerParams(
-            collective_id=0, has_side_effects=True, vmem_limit_bytes=48 * 1024 * 1024
+            collective_id=0, has_side_effects=True, vmem_limit_bytes=60 * 1024 * 1024
         ),
     )(
         reach.reshape(NB * HX, SL),

time: 83 us -> 69.4 us (0.84)
  Pallas kernels: 72.3 us -> 65 us
  local copies, waits for them, and re-layouts: 9.56 us -> 3.53 us
    pallas_call x1, Pallas kernels: 72.3 us -> 65 us  [local(): pl.pallas_call(kernel, name='prox', out_shape=(jax.ShapeDtypeStruct((HX,...]
    unnamed x20 -> x2, local copies, waits for them, and re-layouts: 9.56 us -> 3.53 us
where the time goes in v2:
time: 69.4 us; the launch traced here: 69.2 us
  Pallas kernels  65 us (94%)
  local copies, waits for them, and re-layouts  3.53 us (5%)
    pallas_call x1, Pallas kernels, local(): pl.pallas_call(kernel, name='prox', out_shape=(jax.ShapeDtypeStruct((HX,...  65 us
    unnamed x2, local copies, waits for them, and re-layouts  3.53 us

profile of v2, /device:TPU:1, one launch (start us, length us, event | category | flops | bytes accessed | tf_op | source)
XLA Modules:
  0.0 69.2 jit_solution(12357511750564114458)
XLA Ops:
  0.6 65.0 %prox.1 = (f32[384,256]{1,0:T(8,128)}, f32[384,256]{1,0:T(8,128)}) custom-call(bf16[3072,256]{1,0:T(8,128)(2,1)} %bitcast.1, bf16[256,1024]{1,0:T(8,128)(2,1)} %payoff.1, s32[8,5]{1,0:T(8,128)} %cards_hbm.1, s32[8,1326]{1,0:T(8,128)} %rank_hbm.1, f32[384,256]{1,0:T(8,128)} %logits_hbm.1, s32[4,64]{1,0:T(4,128)} %counts_hbm.1, s32[4,64]{1,0:T(4,128)} %parents_hbm.1, ...), custom_call_target="tpu_custom_call" | custom-call | tf_op jit(solution)/shard_map/prox/pallas_call | solution.py:479
  65.7 1.8 %copy.13 = f32[384,256]{1,0:T(8,128)} copy(f32[384,256]{1,0:T(8,128)} %get-tuple-element.4) | data formatting | bytes 786432
  67.4 1.8 %copy.14 = f32[384,256]{1,0:T(8,128)} copy(f32[384,256]{1,0:T(8,128)} %get-tuple-element.5) | data formatting | bytes 786432

commit v3 on v2

--- a/solution.py
+++ b/solution.py
@@ -15,21 +15,29 @@
 NJ = 8
 HX = 384
 HP = NX * HX
-HJ = HX // NJ
-HZ = HJ // NZ
+HY = HX // 2
+HZ = HY // NZ
+HD = HZ // NL
+PAD = 16
 SL = 256
 SX = NL * SL
 NB = 8
 BOUND = float(NB * HX)
 SCALE = 32767.0 / BOUND
+LIVE = 45 * 44 // 2
+BOUND_PLANE = float(2 * NB * LIVE)
+SCALE_PLANE = 32700.0 / BOUND_PLANE
 MESH = pl.DeviceIdType.MESH
 NEAR = (1, -1, 2, -2)
 UP = (3, 4, 6, 7, 8)
 DOWN = (-3, -4, -6, -7)
 HUB = 5
-PEERS = (1, -1, 2, -2, 3, -3, 5, -5)
+FAR_FIRST = (8, 7, -7, 6, -6, 5, -5, 4, -4, 3, -3, 2, -2, 1, -1)
+GREET = (1, -1, 3, -3, 4, -4)
+PASS_ON = (3, -3, 4, -4)
 PLACES = (0, 1, -1, 2, -2, 5, -5, 3, 4, 6, 7, 8, -3, -4, -6, -7)
 EARLY = 7
+OWNERS = ((1, 2), (0, 2), (1, 1), (1, 3), (0, 1), (0, 3), (1, 0))
 NAN = float("nan")
 
 
@@ -105,9 +113,11 @@
     rows8,
     logit8,
     pay,
+    logit_tiles,
     logit_rows,
-    logit_tiles,
-    mid2,
+    total2,
+    out5,
+    in5,
     in3,
     in4,
     shifts,
@@ -121,10 +131,11 @@
     recv3,
     send4,
     recv4,
-    send_p,
-    recv_p,
+    send5,
+    recv5,
     send_l,
     recv_l,
+    know,
 ):
     board = lax.axis_index("board")
     depth = lax.axis_index("depth")
@@ -153,7 +164,7 @@
                 (table_hbm, table),
                 (onehot_hbm, onehot),
                 (reach_hbm, reach),
-                (payoff, pay.at[depth]),
+                (payoff, pay),
                 (logits_hbm, logits),
                 (counts_hbm, counts),
                 (parents_hbm, parents),
@@ -163,14 +174,18 @@
     for one in loads:
         one.start()
 
+    def owner(other, hop):
+        return (y_lo + other) % 2 * NL + depth, (x + hop) % NX
+
     barrier = pltpu.get_barrier_semaphore()
-
-    @pl.loop(1, NX * NJ)
-    def _(step):
-        other = (x * NJ + j + step) % (NX * NJ)
-        pl.semaphore_signal(barrier, inc=1, device_id=device(z, other % NJ, other // NJ), device_id_type=MESH)
-
-    for dz in PEERS:
+    for other, hop in OWNERS:
+        to_j, to_x = owner(other, hop)
+        pl.semaphore_signal(barrier, inc=1, device_id=device(z, to_j, to_x), device_id_type=MESH)
+    for other in range(2):
+        for step in range(1, NL):
+            to_j = (y_lo + other) % 2 * NL + (depth + step) % NL
+            pl.semaphore_signal(barrier, inc=1, device_id=device(z, to_j, x), device_id_type=MESH)
+    for dz in GREET:
         pl.semaphore_signal(barrier, inc=1, device_id=device(along(dz), j, x), device_id_type=MESH)
 
     for one in loads[:3]:
@@ -214,53 +229,47 @@
 
     @pl.loop(0, NX)
     def _(i):
-        out1[i] = partial(i).reshape(NJ, HJ, SL)
-
-    pl.semaphore_wait(barrier, NX * NJ - 1 + len(PEERS))
-
-    me1 = depth * NJ + x * 2 + y_lo
-
-    def row_copy(step):
-        turn = step // NX
-        to_y_lo = (y_lo + (turn // 2 + 1) // 2) % 2
-        to_y_hi = (depth // 2 + 1 - turn // 4) % 2
-        to_core = (depth + 1 - turn % 2) % 2
-        to_j = to_y_lo * NL + to_y_hi * 2 + to_core
-        hop = step % NX
-        to_x = (x + 2 + hop + hop * (hop - 1) // 2) % NX
+        out1[i] = partial(i).reshape(2, HY, SL)
+
+    pl.semaphore_wait(barrier, len(OWNERS) + 2 * (NL - 1) + len(GREET))
+    for dz in PASS_ON:
+        pl.semaphore_signal(know, inc=1, device_id=device(along(dz), j, x), device_id_type=MESH)
+
+    me1 = x * 2 + y_lo
+
+    def copy1(i):
+        to_j, to_x = owner(*OWNERS[i])
         return copy(
-            out1.at[to_x, to_j], in1.at[me1], send1.at[step], recv1.at[me1], device(z, to_j, to_x)
-        )
-
-    @pl.loop(0, NX * NJ - 1)
-    def _(step):
-        row_copy(step).start()
-
-    in1[me1] = out1[x, j]
+            out1.at[to_x, to_j // NL], in1.at[me1], send1.at[i], recv1.at[me1], device(z, to_j, to_x)
+        )
+
+    for i in range(len(OWNERS)):
+        copy1(i).start()
+    in1[me1] = out1[x, y_lo]
 
     for one in loads[5:]:
         one.wait()
 
+    for half in range(2):
+        logit_tiles[:, half, :] = logits[:, half * 128 : half * 128 + 128]
+
     def depth_peer(step):
         return (depth + step) % NL
 
-    for step in range(1, NL):
-        to = y_lo * NL + depth_peer(step)
-        copy(
-            logits.at[pl.ds(pl.multiple_of(to * HJ, HJ), HJ)],
+    def copy_l(step):
+        to = depth_peer(step)
+        rows = pl.ds(y_lo * HY + z * HZ + to * HD, HD)
+        return copy(
+            logit_tiles.at[rows],
             logit_rows.at[depth],
             send_l.at[step],
             recv_l.at[depth],
-            device(z, to, x),
-        ).start()
-    logit_rows[depth] = logits[pl.ds(pl.multiple_of(j * HJ, HJ), HJ), :]
-    across = depth_peer(2)
-    beside = depth + 1 - 2 * (depth % 2)
-    opposite = across + 1 - 2 * (across % 2)
-    pay_across = copy(pay.at[depth], pay.at[depth], send_p.at[0], recv_p.at[depth], device(z, y_lo * NL + across, x))
-    pay_across.start()
-    pay_beside = copy(pay.at[depth], pay.at[depth], send_p.at[1], recv_p.at[depth], device(z, y_lo * NL + beside, x))
-    pay_beside.start()
+            device(z, y_lo * NL + to, x),
+        )
+
+    for step in range(1, NL):
+        copy_l(step).start()
+    logit_rows[depth] = logit_tiles[pl.ds(y_lo * HY + z * HZ + depth * HD, HD)]
 
     spread = (
         lax.broadcasted_iota(jnp.int32, (SL // ACT, SL), 0)
@@ -279,90 +288,79 @@
     for level in range(NL):
         owners[level] = jnp.where(seq == parents_wide[level : level + 1, :], 1.0, 0.0).astype(jnp.bfloat16)
 
-    @pl.loop(1, NX * NJ)
-    def _(step):
-        slot = (me1 + step) % (NX * NJ)
-        copy(in1.at[slot], in1.at[slot], send1.at[0], recv1.at[slot], device(z, (j + 1) % NJ, x)).wait_recv()
-
-    for block in range(NL):
-        total = in1[block * NJ].astype(jnp.int32)
-        for source in range(1, NJ):
-            total += in1[block * NJ + source].astype(jnp.int32)
-        total = total.astype(jnp.float32)
-        out2[:, 2 * block, :] = total[:, :128]
-        out2[:, 2 * block + 1, :] = total[:, 128:]
-
-    def block2(dz):
-        return out2.at[pl.ds(along(dz) * HZ, HZ)]
-
-    sums = []
-    for i, k in enumerate(UP):
-        sums.append((block2(-k), i, HUB - k))
-    for i, k in enumerate(DOWN):
-        sums.append((block2(-k), len(UP) + i, -HUB - k))
-    for i, dz in enumerate(NEAR):
-        sums.append((block2(dz), len(UP) + len(DOWN) + i, dz))
-
-    def copy2(src, slot, dz):
-        return copy(src, in2.at[slot], send2.at[slot], recv2.at[slot], device(along(dz), j, x))
-
-    for src, slot, dz in sums:
-        copy2(src, slot, dz).start()
-
-    def wait2(slots):
-        total = None
-        for slot in slots:
-            copy2(in2.at[slot], slot, 1).wait_recv()
-        for slot in slots:
-            total = in2[slot] if total is None else total + in2[slot]
-        return total
-
-    n_up, n_far = len(UP), len(UP) + len(DOWN)
-    n_all = n_far + len(NEAR)
-    mid2[0] = wait2(range(n_up)) + out2[pl.ds(along(-HUB) * HZ, HZ)]
-    copy2(mid2.at[0], n_all, -HUB).start()
-    mid2[1] = wait2(range(n_up, n_far)) + out2[pl.ds(along(HUB) * HZ, HZ)]
-    copy2(mid2.at[1], n_all + 1, HUB).start()
-
-    copy(pay.at[depth], pay.at[across], send_p.at[0], recv_p.at[across], device(z, (j + 1) % NJ, x)).wait_recv()
-    pay_on = copy(
-        pay.at[across], pay.at[across], send_p.at[2], recv_p.at[across], device(z, y_lo * NL + beside, x)
-    )
-    pay_on.start()
-    copy(pay.at[depth], pay.at[beside], send_p.at[0], recv_p.at[beside], device(z, (j + 1) % NJ, x)).wait_recv()
-    copy(pay.at[depth], pay.at[opposite], send_p.at[0], recv_p.at[opposite], device(z, (j + 1) % NJ, x)).wait_recv()
+    for i in range(len(OWNERS)):
+        slot = (me1 + 1 + i) % NJ
+        copy(in1.at[slot], in1.at[slot], send1.at[0], recv1.at[slot], device(z, j, (x + 1) % NX)).wait_recv()
+
+    total = in1[0].astype(jnp.int32)
+    for source in range(1, NJ):
+        total += in1[source].astype(jnp.int32)
+    total2[:HY, :] = total.astype(jnp.float32) * (SCALE_PLANE / SCALE)
+    total2[HY:, :] = jnp.zeros((8, SL), jnp.float32)
+    for to_z in range(NZ):
+        rows = jnp.round(total2[to_z * HZ : to_z * HZ + PAD, :])
+        out2[to_z] = rows.astype(jnp.int32).astype(jnp.int16)
+
+    pl.semaphore_wait(know, len(PASS_ON))
+
+    def copy2(i):
+        dz = FAR_FIRST[i]
+        return copy(
+            out2.at[along(dz)], in2.at[i], send2.at[i], recv2.at[i], device(along(dz), j, x)
+        )
+
+    for i in range(NZ - 1):
+        copy2(i).start()
 
     rows8[...] = jnp.zeros((8, SX), jnp.float32)
     logit8[...] = jnp.zeros((8, SX), jnp.float32)
     for step in range(1, NL):
         slot = depth_peer(step)
         copy(
-            logit_rows.at[slot], logit_rows.at[slot], send_l.at[0], recv_l.at[slot], device(z, (j + 1) % NJ, x)
+            logit_rows.at[slot], logit_rows.at[slot], send_l.at[0], recv_l.at[slot], device(z, j, (x + 1) % NX)
         ).wait_recv()
     for group in range(8):
-        logit_tiles[:, group, :] = logit_rows[group // 2, :, (group % 2) * 128 : (group % 2) * 128 + 128]
-    for group in range(8):
-        logit8[0:HZ, group * 128 : (group + 1) * 128] = logit_tiles[pl.ds(z * HZ, HZ), group, :]
-
-    mid2[2] = wait2(range(n_far, n_all + 2)) + out2[pl.ds(z * HZ, HZ)]
-    for group in range(8):
-        rows8[0:HZ, group * 128 : (group + 1) * 128] = mid2[2, :, group, :]
-    counter = rows8[...]
+        logit8[0:HD, group * 128 : (group + 1) * 128] = logit_rows[group // 2, :, group % 2, :]
+
+    for i in range(NZ - 1):
+        copy2(i).wait_recv()
+    total = out2[z].astype(jnp.int32)
+    for i in range(NZ - 1):
+        total += in2[i].astype(jnp.int32)
+    counter = total.astype(jnp.float32)
     high = counter.astype(jnp.bfloat16).astype(jnp.float32)
     both = jnp.concatenate([high, counter - high], axis=0).astype(jnp.bfloat16)
-    gradient = jnp.dot(both[:, :SL], pay[0], preferred_element_type=jnp.float32)
-    for block in range(1, NL):
-        gradient += jnp.dot(
-            both[:, block * SL : (block + 1) * SL], pay[block], preferred_element_type=jnp.float32
-        )
-    gradient = (gradient[:8] + gradient[8:]) * (1.0 / SCALE)
+    partial_gradient = jnp.dot(both, pay[...], preferred_element_type=jnp.float32)
+    partial_gradient = (partial_gradient[:PAD] + partial_gradient[PAD:]) * (1.0 / SCALE_PLANE)
+    for group in range(8):
+        out5[:, group, :] = partial_gradient[:HZ, group * 128 : (group + 1) * 128]
+
+    def copy5(step):
+        to = depth_peer(step)
+        return copy(
+            out5.at[pl.ds(to * HD, HD)],
+            in5.at[step],
+            send5.at[step],
+            recv5.at[step],
+            device(z, y_lo * NL + to, x),
+        )
+
+    for step in range(1, NL):
+        copy5(step).start()
+    for step in range(1, NL):
+        copy5(step).wait_recv()
+    total = out5[pl.ds(depth * HD, HD)] + in5[1] + in5[2] + in5[3]
+    in5[0] = total
+    for group in range(8):
+        rows8[0:HD, group * 128 : (group + 1) * 128] = in5[0, :, group, :]
+    gradient = rows8[...]
 
     incoming = jnp.zeros((8, SL), jnp.float32)
     for level in range(NL - 1, -1, -1):
         cols = slice(level * SL, (level + 1) * SL)
         shift = gradient[:, cols] + incoming
-        in3[0, level, :, 0, :] = shift[:HZ, :128]
-        in3[0, level, :, 1, :] = shift[:HZ, 128:]
+        in3[0, level, :, 0, :] = shift[:HD, :128]
+        in3[0, level, :, 1, :] = shift[:HD, 128:]
         if level:
             value = group_value(logit8[:, cols] + shift, legal[level : level + 1, :])
             incoming = hand_down(value, owners[level])
@@ -415,7 +413,7 @@
 
     def place(from_j, block, slots):
         for slot in slots:
-            rows = pl.ds((from_j * NZ + along(PLACES[slot])) * HZ, HZ)
+            rows = pl.ds(from_j // NL * HY + along(PLACES[slot]) * HZ + from_j % NL * HD, HD)
             shifts[rows] = block(slot)
 
     place(j, lambda slot: in3[slot, depth], range(NZ))
@@ -441,14 +439,13 @@
     policy[...] = jnp.where(can > 0.0, scores - value, 0.0)
     passed[...] = hand_down(value, owners[depth])
 
-    @pl.loop(0, NX * NJ - 1)
-    def _(step):
-        row_copy(step).wait_send()
-
-    for src, slot, dz in sums:
-        copy2(src, slot, dz).wait_send()
-    copy2(mid2.at[0], n_all, -HUB).wait_send()
-    copy2(mid2.at[1], n_all + 1, HUB).wait_send()
+    for i in range(len(OWNERS)):
+        copy1(i).wait_send()
+    for i in range(NZ - 1):
+        copy2(i).wait_send()
+    for step in range(1, NL):
+        copy5(step).wait_send()
+        copy_l(step).wait_send()
     for one in straight + onward + onward_down:
         one.wait_send()
 
@@ -456,19 +453,6 @@
     def _(step):
         copy4(step, 0).wait_send()
         copy4(step, 1).wait_send()
-
-    for step in range(1, NL):
-        to = y_lo * NL + depth_peer(step)
-        copy(
-            logits.at[pl.ds(pl.multiple_of(to * HJ, HJ), HJ)],
-            logit_rows.at[depth],
-            send_l.at[step],
-            recv_l.at[depth],
-            device(z, to, x),
-        ).wait_send()
-    pay_across.wait_send()
-    pay_beside.wait_send()
-    pay_on.wait_send()
 
 
 def local(reach, payoff, board_cards, hand_rank, logits, action_counts, parent_seq):
@@ -494,33 +478,36 @@
             dma((9,)),
             pltpu.VMEM((NB, HP), f32),
             pltpu.VMEM((HP, NB), f32),
-            pltpu.VMEM((NX, NJ, HJ, SL), i16),
-            pltpu.VMEM((NL * NJ, HJ, SL), i16),
-            pltpu.VMEM((HJ, 8, 128), f32),
-            pltpu.VMEM((NZ, HZ, 8, 128), f32),
+            pltpu.VMEM((NX, 2, HY, SL), i16),
+            pltpu.VMEM((NJ, HY, SL), i16),
+            pltpu.VMEM((NZ, PAD, SL), i16),
+            pltpu.VMEM((NZ - 1, PAD, SL), i16),
             pltpu.VMEM((8, SX), f32),
             pltpu.VMEM((8, SX), f32),
-            pltpu.VMEM((NL, SL, SX), bf16),
-            pltpu.VMEM((NL, HJ, SL), f32),
-            pltpu.VMEM((HJ, 8, 128), f32),
-            pltpu.VMEM((3, HZ, 8, 128), f32),
-            pltpu.VMEM((NZ, NL, HZ, 2, 128), f32),
-            pltpu.VMEM((NJ, NZ, HZ, 2, 128), f32),
+            pltpu.VMEM((SL, SX), bf16),
+            pltpu.VMEM((HX, 2, 128), f32),
+            pltpu.VMEM((NL, HD, 2, 128), f32),
+            pltpu.VMEM((HY + 8, SL), f32),
+            pltpu.VMEM((HZ, 8, 128), f32),
+            pltpu.VMEM((NL, HD, 8, 128), f32),
+            pltpu.VMEM((NZ, NL, HD, 2, 128), f32),
+            pltpu.VMEM((NJ, NZ, HD, 2, 128), f32),
             pltpu.VMEM((HX, 2, 128), f32),
             pltpu.VMEM((NL, SL), f32),
             pltpu.VMEM((NL, SL, SL), bf16),
-            dma((NX * NJ,)),
-            dma((NL * NJ,)),
-            dma((NZ,)),
-            dma((NZ,)),
+            dma((len(OWNERS),)),
+            dma((NJ,)),
+            dma((NZ - 1,)),
+            dma((NZ - 1,)),
             dma((NZ,)),
             dma((NZ,)),
             dma((2, NJ)),
             dma((2, NJ)),
-            dma((3,)),
             dma((NL,)),
             dma((NL,)),
             dma((NL,)),
+            dma((NL,)),
+            pltpu.SemaphoreType.REGULAR,
         ],
         compiler_params=pltpu.CompilerParams(
             collective_id=0, has_side_effects=True, vmem_limit_bytes=60 * 1024 * 1024

time: 69.4 us -> 64.1 us (0.924)
  Pallas kernels: 65 us -> 59.7 us
    pallas_call x1, Pallas kernels: 65 us -> 59.7 us  [local(): pl.pallas_call(kernel, name='prox', out_shape=(jax.ShapeDtypeStruct((HX,...]
where the time goes in v3:
time: 64.1 us; the launch traced here: 63.9 us
  Pallas kernels  59.7 us (93%)
  local copies, waits for them, and re-layouts  3.53 us (6%)
    pallas_call x1, Pallas kernels, local(): pl.pallas_call(kernel, name='prox', out_shape=(jax.ShapeDtypeStruct((HX,...  59.7 us
    unnamed x2, local copies, waits for them, and re-layouts  3.53 us

profile of v3, /device:TPU:1, one launch (start us, length us, event | category | flops | bytes accessed | tf_op | source)
XLA Modules:
  0.0 63.9 jit_solution(8517032787153999192)
XLA Ops:
  0.6 59.7 %prox.1 = (f32[384,256]{1,0:T(8,128)}, f32[384,256]{1,0:T(8,128)}) custom-call(bf16[3072,256]{1,0:T(8,128)(2,1)} %bitcast.1, bf16[256,1024]{1,0:T(8,128)(2,1)} %payoff.1, s32[8,5]{1,0:T(8,128)} %cards_hbm.1, s32[8,1326]{1,0:T(8,128)} %rank_hbm.1, f32[384,256]{1,0:T(8,128)} %logits_hbm.1, s32[4,64]{1,0:T(4,128)} %counts_hbm.1, s32[4,64]{1,0:T(4,128)} %parents_hbm.1, ...), custom_call_target="tpu_custom_call" | custom-call | tf_op jit(solution)/shard_map/prox/pallas_call | solution.py:463
  60.3 1.8 %copy.13 = f32[384,256]{1,0:T(8,128)} copy(f32[384,256]{1,0:T(8,128)} %get-tuple-element.4) | data formatting | bytes 786432
  62.1 1.8 %copy.14 = f32[384,256]{1,0:T(8,128)} copy(f32[384,256]{1,0:T(8,128)} %get-tuple-element.5) | data formatting | bytes 786432

commit v4 on v3

--- a/solution.py
+++ b/solution.py
@@ -33,11 +33,10 @@
 DOWN = (-3, -4, -6, -7)
 HUB = 5
 FAR_FIRST = (8, 7, -7, 6, -6, 5, -5, 4, -4, 3, -3, 2, -2, 1, -1)
-GREET = (1, -1, 3, -3, 4, -4)
-PASS_ON = (3, -3, 4, -4)
-PLACES = (0, 1, -1, 2, -2, 5, -5, 3, 4, 6, 7, 8, -3, -4, -6, -7)
-EARLY = 7
-OWNERS = ((1, 2), (0, 2), (1, 1), (1, 3), (0, 1), (0, 3), (1, 0))
+GREET = (1, -1, 2, -2)
+PLACES = (0, 1, -1, 2, -2, 5, -5, -3, -4, -6, -7, 3, 4, 6, 7, 8)
+PARTS = ((0, 7), (7, 11), (11, 16))
+ROW_PEERS = 2 * NX - 1
 NAN = float("nan")
 
 
@@ -174,13 +173,14 @@
     for one in loads:
         one.start()
 
-    def owner(other, hop):
-        return (y_lo + other) % 2 * NL + depth, (x + hop) % NX
+    def hop_x(i):
+        return (x + 2 + i + i * (i - 1) // 2) % NX
 
     barrier = pltpu.get_barrier_semaphore()
-    for other, hop in OWNERS:
-        to_j, to_x = owner(other, hop)
-        pl.semaphore_signal(barrier, inc=1, device_id=device(z, to_j, to_x), device_id_type=MESH)
+    for i in range(NX):
+        for other in range(1 if i == NX - 1 else 0, 2):
+            to_j = (y_lo + other) % 2 * NL + depth
+            pl.semaphore_signal(barrier, inc=1, device_id=device(z, to_j, hop_x(i)), device_id_type=MESH)
     for other in range(2):
         for step in range(1, NL):
             to_j = (y_lo + other) % 2 * NL + (depth + step) % NL
@@ -227,24 +227,40 @@
             )
         return jnp.round(total * SCALE).astype(jnp.int32).astype(jnp.int16)
 
+    me1 = x * 2 + y_lo
+
+    def copy1(i, other):
+        to_x, to_y = hop_x(i), (y_lo + other) % 2
+        return copy(
+            out1.at[to_x, to_y],
+            in1.at[me1],
+            send1.at[i, other],
+            recv1.at[me1],
+            device(z, to_y * NL + depth, to_x),
+        )
+
     @pl.loop(0, NX)
     def _(i):
-        out1[i] = partial(i).reshape(2, HY, SL)
-
-    pl.semaphore_wait(barrier, len(OWNERS) + 2 * (NL - 1) + len(GREET))
-    for dz in PASS_ON:
-        pl.semaphore_signal(know, inc=1, device_id=device(along(dz), j, x), device_id_type=MESH)
-
-    me1 = x * 2 + y_lo
-
-    def copy1(i):
-        to_j, to_x = owner(*OWNERS[i])
-        return copy(
-            out1.at[to_x, to_j // NL], in1.at[me1], send1.at[i], recv1.at[me1], device(z, to_j, to_x)
-        )
-
-    for i in range(len(OWNERS)):
-        copy1(i).start()
+        to_x = hop_x(i)
+        out1[to_x] = partial(to_x).reshape(2, HY, SL)
+
+        @pl.when(i == 0)
+        def _():
+            pl.semaphore_wait(barrier, ROW_PEERS + 2 * (NL - 1) + len(GREET))
+            for dz in (2, -2):
+                pl.semaphore_signal(
+                    know.at[0], inc=1, device_id=device(along(dz), j, x), device_id_type=MESH
+                )
+
+        copy1(i, 1).start()
+
+        @pl.when(i < NX - 1)
+        def _():
+            copy1(i, 0).start()
+
+    pl.semaphore_wait(know.at[0], 2)
+    for dz in (4, -4):
+        pl.semaphore_signal(know.at[1], inc=1, device_id=device(along(dz), j, x), device_id_type=MESH)
     in1[me1] = out1[x, y_lo]
 
     for one in loads[5:]:
@@ -288,9 +304,9 @@
     for level in range(NL):
         owners[level] = jnp.where(seq == parents_wide[level : level + 1, :], 1.0, 0.0).astype(jnp.bfloat16)
 
-    for i in range(len(OWNERS)):
+    for i in range(ROW_PEERS):
         slot = (me1 + 1 + i) % NJ
-        copy(in1.at[slot], in1.at[slot], send1.at[0], recv1.at[slot], device(z, j, (x + 1) % NX)).wait_recv()
+        copy(in1.at[slot], in1.at[slot], send1.at[0, 0], recv1.at[slot], device(z, j, (x + 1) % NX)).wait_recv()
 
     total = in1[0].astype(jnp.int32)
     for source in range(1, NJ):
@@ -301,7 +317,7 @@
         rows = jnp.round(total2[to_z * HZ : to_z * HZ + PAD, :])
         out2[to_z] = rows.astype(jnp.int32).astype(jnp.int16)
 
-    pl.semaphore_wait(know, len(PASS_ON))
+    pl.semaphore_wait(know.at[1], 2)
 
     def copy2(i):
         dz = FAR_FIRST[i]
@@ -345,7 +361,7 @@
             device(z, y_lo * NL + to, x),
         )
 
-    for step in range(1, NL):
+    for step in (2, 1, 3):
         copy5(step).start()
     for step in range(1, NL):
         copy5(step).wait_recv()
@@ -387,7 +403,7 @@
         one.start()
 
     def copy4(step, part):
-        slots = pl.ds(0, EARLY) if part == 0 else pl.ds(EARLY, NZ - EARLY)
+        slots = pl.ds(PARTS[part][0], PARTS[part][1] - PARTS[part][0])
         to_j = (j + step) % NJ
         return copy(
             in3.at[slots, to_j % NL],
@@ -397,19 +413,14 @@
             device(z, to_j, x),
         )
 
-    for source in NEAR:
-        wait3(source)
-
-    @pl.loop(1, NJ)
-    def _(step):
-        copy4(step, 0).start()
-
-    for source in PLACES[EARLY:]:
-        wait3(source)
-
-    @pl.loop(1, NJ)
-    def _(step):
-        copy4(step, 1).start()
+    for part, (begin, end) in enumerate(PARTS):
+        for slot in range(begin, end):
+            if PLACES[slot] not in (0, HUB, -HUB):
+                wait3(PLACES[slot])
+
+        @pl.loop(1, NJ)
+        def _(step):
+            copy4(step, part).start()
 
     def place(from_j, block, slots):
         for slot in slots:
@@ -418,8 +429,8 @@
 
     place(j, lambda slot: in3[slot, depth], range(NZ))
 
-    for part, slots in enumerate((range(EARLY), range(EARLY, NZ))):
-        whole = pl.ds(slots[0], len(slots))
+    for part, (begin, end) in enumerate(PARTS):
+        whole = pl.ds(begin, end - begin)
 
         @pl.loop(1, NJ)
         def _(step):
@@ -431,7 +442,7 @@
                 recv4.at[part, slot],
                 device(z, slot, x),
             ).wait_recv()
-            place(slot, lambda one: in4[slot, one], slots)
+            place(slot, lambda one: in4[slot, one], range(begin, end))
 
     scores = logits[...] + jnp.concatenate([shifts[:, 0, :], shifts[:, 1, :]], axis=1)
     can = legal[pl.ds(depth, 1), :]
@@ -439,8 +450,9 @@
     policy[...] = jnp.where(can > 0.0, scores - value, 0.0)
     passed[...] = hand_down(value, owners[depth])
 
-    for i in range(len(OWNERS)):
-        copy1(i).wait_send()
+    for i in range(NX):
+        for other in range(1 if i == NX - 1 else 0, 2):
+            copy1(i, other).wait_send()
     for i in range(NZ - 1):
         copy2(i).wait_send()
     for step in range(1, NL):
@@ -451,8 +463,8 @@
 
     @pl.loop(1, NJ)
     def _(step):
-        copy4(step, 0).wait_send()
-        copy4(step, 1).wait_send()
+        for part in range(len(PARTS)):
+            copy4(step, part).wait_send()
 
 
 def local(reach, payoff, board_cards, hand_rank, logits, action_counts, parent_seq):
@@ -495,33 +507,38 @@
             pltpu.VMEM((HX, 2, 128), f32),
             pltpu.VMEM((NL, SL), f32),
             pltpu.VMEM((NL, SL, SL), bf16),
-            dma((len(OWNERS),)),
+            dma((NX, 2)),
             dma((NJ,)),
             dma((NZ - 1,)),
             dma((NZ - 1,)),
             dma((NZ,)),
             dma((NZ,)),
-            dma((2, NJ)),
-            dma((2, NJ)),
+            dma((len(PARTS), NJ)),
+            dma((len(PARTS), NJ)),
             dma((NL,)),
             dma((NL,)),
             dma((NL,)),
             dma((NL,)),
-            pltpu.SemaphoreType.REGULAR,
+            pltpu.SemaphoreType.REGULAR((2,)),
         ],
         compiler_params=pltpu.CompilerParams(
-            collective_id=0, has_side_effects=True, vmem_limit_bytes=60 * 1024 * 1024
+            collective_id=0, has_side_effects=True, vmem_limit_bytes=32 * 1024 * 1024
         ),
     )(
-        reach.reshape(NB * HX, SL),
-        payoff,
-        board_cards,
-        hand_rank,
-        logits,
-        action_counts,
-        parent_seq,
-        jnp.asarray(table),
-        jnp.asarray(onehot, jnp.bfloat16),
+        *[
+            pltpu.with_memory_space_constraint(operand, pltpu.HBM)
+            for operand in (
+                reach.reshape(NB * HX, SL),
+                payoff,
+                board_cards,
+                hand_rank,
+                logits,
+                action_counts,
+                parent_seq,
+                jnp.asarray(table),
+                jnp.asarray(onehot, jnp.bfloat16),
+            )
+        ]
     )
 
 

time: 64.1 us -> 58.8 us (0.917)
  Pallas kernels: 59.7 us -> 56.5 us
  local copies, waits for them, and re-layouts: 3.53 us -> 1.49 us
    pallas_call x1, Pallas kernels: 59.7 us -> 56.5 us  [local(): pl.pallas_call(kernel, name='prox', out_shape=(jax.ShapeDtypeStruct((HX,...]
    unnamed x2, local copies, waits for them, and re-layouts: 3.53 us -> 1.49 us
where the time goes in v4:
time: 58.8 us; the launch traced here: 58.7 us
  Pallas kernels  56.5 us (96%)
  local copies, waits for them, and re-layouts  1.49 us (3%)
  between operations  0.64 us (1%)
    pallas_call x1, Pallas kernels, local(): pl.pallas_call(kernel, name='prox', out_shape=(jax.ShapeDtypeStruct((HX,...  56.5 us
    unnamed x2, local copies, waits for them, and re-layouts  1.49 us

profile of v4, /device:TPU:1, one launch (start us, length us, event | category | flops | bytes accessed | tf_op | source)
XLA Modules:
  0.0 58.7 jit_solution(5859321564571113002)
XLA Ops:
  0.6 56.5 %prox.1 = (f32[384,256]{1,0:T(8,128)S(1)}, f32[384,256]{1,0:T(8,128)S(1)}) custom-call(bf16[3072,256]{1,0:T(8,128)(2,1)} %bitcast.1, bf16[256,1024]{1,0:T(8,128)(2,1)} %payoff.1, s32[8,5]{1,0:T(8,128)} %cards_hbm.1, s32[8,1326]{1,0:T(8,128)} %rank_hbm.1, f32[384,256]{1,0:T(8,128)} %logits_hbm.1, s32[4,64]{1,0:T(4,128)} %counts_hbm.1, s32[4,64]{1,0:T(4,128)} %parents_hbm.1, ...), custom_call_target="tpu_custom_call" | custom-call | tf_op jit(solution)/shard_map/prox/pallas_call | solution.py:475
  57.2 0.7 %copy.13 = f32[384,256]{1,0:T(8,128)} copy(f32[384,256]{1,0:T(8,128)S(1)} %get-tuple-element.4) | data formatting | bytes 786432
  57.9 0.7 %copy.14 = f32[384,256]{1,0:T(8,128)} copy(f32[384,256]{1,0:T(8,128)S(1)} %get-tuple-element.5) | data formatting | bytes 786432

commit v5 on v4

--- a/solution.py
+++ b/solution.py
@@ -17,7 +17,6 @@
 HP = NX * HX
 HY = HX // 2
 HZ = HY // NZ
-HD = HZ // NL
 PAD = 16
 SL = 256
 SX = NL * SL
@@ -37,6 +36,7 @@
 PLACES = (0, 1, -1, 2, -2, 5, -5, -3, -4, -6, -7, 3, 4, 6, 7, 8)
 PARTS = ((0, 7), (7, 11), (11, 16))
 ROW_PEERS = 2 * NX - 1
+CHUNKS = 3
 NAN = float("nan")
 
 
@@ -92,8 +92,9 @@
     parents_hbm,
     table_hbm,
     onehot_hbm,
-    policy,
-    passed,
+    scores,
+    own_legal,
+    own_owner,
     reach,
     cards,
     rank,
@@ -109,14 +110,15 @@
     in1,
     out2,
     in2,
-    rows8,
-    logit8,
+    rows16,
+    logit16,
     pay,
     logit_tiles,
     logit_rows,
     total2,
     out5,
     in5,
+    out3,
     in3,
     in4,
     shifts,
@@ -181,10 +183,9 @@
         for other in range(1 if i == NX - 1 else 0, 2):
             to_j = (y_lo + other) % 2 * NL + depth
             pl.semaphore_signal(barrier, inc=1, device_id=device(z, to_j, hop_x(i)), device_id_type=MESH)
-    for other in range(2):
-        for step in range(1, NL):
-            to_j = (y_lo + other) % 2 * NL + (depth + step) % NL
-            pl.semaphore_signal(barrier, inc=1, device_id=device(z, to_j, x), device_id_type=MESH)
+    for step in range(1, NL):
+        to_j = y_lo * NL + (depth + step) % NL
+        pl.semaphore_signal(barrier, inc=1, device_id=device(z, to_j, x), device_id_type=MESH)
     for dz in GREET:
         pl.semaphore_signal(barrier, inc=1, device_id=device(along(dz), j, x), device_id_type=MESH)
 
@@ -246,7 +247,7 @@
 
         @pl.when(i == 0)
         def _():
-            pl.semaphore_wait(barrier, ROW_PEERS + 2 * (NL - 1) + len(GREET))
+            pl.semaphore_wait(barrier, ROW_PEERS + NL - 1 + len(GREET))
             for dz in (2, -2):
                 pl.semaphore_signal(
                     know.at[0], inc=1, device_id=device(along(dz), j, x), device_id_type=MESH
@@ -274,9 +275,8 @@
 
     def copy_l(step):
         to = depth_peer(step)
-        rows = pl.ds(y_lo * HY + z * HZ + to * HD, HD)
         return copy(
-            logit_tiles.at[rows],
+            logit_tiles.at[pl.ds(y_lo * HY + z * HZ, HZ)],
             logit_rows.at[depth],
             send_l.at[step],
             recv_l.at[depth],
@@ -285,7 +285,7 @@
 
     for step in range(1, NL):
         copy_l(step).start()
-    logit_rows[depth] = logit_tiles[pl.ds(y_lo * HY + z * HZ + depth * HD, HD)]
+    logit_rows[depth] = logit_tiles[pl.ds(y_lo * HY + z * HZ, HZ)]
 
     spread = (
         lax.broadcasted_iota(jnp.int32, (SL // ACT, SL), 0)
@@ -304,13 +304,13 @@
     for level in range(NL):
         owners[level] = jnp.where(seq == parents_wide[level : level + 1, :], 1.0, 0.0).astype(jnp.bfloat16)
 
+    total = in1[me1].astype(jnp.int32)
     for i in range(ROW_PEERS):
         slot = (me1 + 1 + i) % NJ
-        copy(in1.at[slot], in1.at[slot], send1.at[0, 0], recv1.at[slot], device(z, j, (x + 1) % NX)).wait_recv()
-
-    total = in1[0].astype(jnp.int32)
-    for source in range(1, NJ):
-        total += in1[source].astype(jnp.int32)
+        copy(
+            in1.at[slot], in1.at[slot], send1.at[0, 0], recv1.at[slot], device(z, j, (x + 1) % NX)
+        ).wait_recv()
+        total += in1[slot].astype(jnp.int32)
     total2[:HY, :] = total.astype(jnp.float32) * (SCALE_PLANE / SCALE)
     total2[HY:, :] = jnp.zeros((8, SL), jnp.float32)
     for to_z in range(NZ):
@@ -328,20 +328,19 @@
     for i in range(NZ - 1):
         copy2(i).start()
 
-    rows8[...] = jnp.zeros((8, SX), jnp.float32)
-    logit8[...] = jnp.zeros((8, SX), jnp.float32)
+    rows16[...] = jnp.zeros((PAD, SX), jnp.float32)
+    logit16[...] = jnp.zeros((PAD, SX), jnp.float32)
     for step in range(1, NL):
         slot = depth_peer(step)
         copy(
             logit_rows.at[slot], logit_rows.at[slot], send_l.at[0], recv_l.at[slot], device(z, j, (x + 1) % NX)
         ).wait_recv()
     for group in range(8):
-        logit8[0:HD, group * 128 : (group + 1) * 128] = logit_rows[group // 2, :, group % 2, :]
-
-    for i in range(NZ - 1):
+        logit16[0:HZ, group * 128 : (group + 1) * 128] = logit_rows[group // 2, :, group % 2, :]
+
+    total = out2[z].astype(jnp.int32)
+    for i in range(NZ - 2, -1, -1):
         copy2(i).wait_recv()
-    total = out2[z].astype(jnp.int32)
-    for i in range(NZ - 1):
         total += in2[i].astype(jnp.int32)
     counter = total.astype(jnp.float32)
     high = counter.astype(jnp.bfloat16).astype(jnp.float32)
@@ -354,7 +353,7 @@
     def copy5(step):
         to = depth_peer(step)
         return copy(
-            out5.at[pl.ds(to * HD, HD)],
+            out5,
             in5.at[step],
             send5.at[step],
             recv5.at[step],
@@ -365,21 +364,23 @@
         copy5(step).start()
     for step in range(1, NL):
         copy5(step).wait_recv()
-    total = out5[pl.ds(depth * HD, HD)] + in5[1] + in5[2] + in5[3]
+    total = out5[...] + in5[1] + in5[2] + in5[3]
     in5[0] = total
     for group in range(8):
-        rows8[0:HD, group * 128 : (group + 1) * 128] = in5[0, :, group, :]
-    gradient = rows8[...]
-
-    incoming = jnp.zeros((8, SL), jnp.float32)
+        rows16[0:HZ, group * 128 : (group + 1) * 128] = in5[0, :, group, :]
+    gradient = rows16[...]
+
+    incoming = jnp.zeros((PAD, SL), jnp.float32)
     for level in range(NL - 1, -1, -1):
         cols = slice(level * SL, (level + 1) * SL)
         shift = gradient[:, cols] + incoming
-        in3[0, level, :, 0, :] = shift[:HD, :128]
-        in3[0, level, :, 1, :] = shift[:HD, 128:]
+        out3[level, :, 0, :] = shift[:HZ, :128]
+        out3[level, :, 1, :] = shift[:HZ, 128:]
         if level:
-            value = group_value(logit8[:, cols] + shift, legal[level : level + 1, :])
+            value = group_value(logit16[:, cols] + shift, legal[level : level + 1, :])
             incoming = hand_down(value, owners[level])
+
+    in3[0] = out3[depth]
 
     def copy3(source, dz):
         slot = PLACES.index(source)
@@ -402,53 +403,34 @@
     for one in onward_down:
         one.start()
 
-    def copy4(step, part):
+    def copy4(part):
         slots = pl.ds(PARTS[part][0], PARTS[part][1] - PARTS[part][0])
-        to_j = (j + step) % NJ
         return copy(
-            in3.at[slots, to_j % NL],
-            in4.at[j, slots],
-            send4.at[part, step],
-            recv4.at[part, j],
-            device(z, to_j, x),
-        )
+            in3.at[slots],
+            in4.at[slots],
+            send4.at[part],
+            recv4.at[part],
+            device(z, (1 - y_lo) * NL + depth, x),
+        )
+
+    def place(block, half, slot):
+        shifts[pl.ds(half * HY + along(PLACES[slot]) * HZ, HZ)] = block[slot]
 
     for part, (begin, end) in enumerate(PARTS):
         for slot in range(begin, end):
             if PLACES[slot] not in (0, HUB, -HUB):
                 wait3(PLACES[slot])
-
-        @pl.loop(1, NJ)
-        def _(step):
-            copy4(step, part).start()
-
-    def place(from_j, block, slots):
-        for slot in slots:
-            rows = pl.ds(from_j // NL * HY + along(PLACES[slot]) * HZ + from_j % NL * HD, HD)
-            shifts[rows] = block(slot)
-
-    place(j, lambda slot: in3[slot, depth], range(NZ))
-
+        copy4(part).start()
+        for slot in range(begin, end):
+            place(in3, y_lo, slot)
     for part, (begin, end) in enumerate(PARTS):
-        whole = pl.ds(begin, end - begin)
-
-        @pl.loop(1, NJ)
-        def _(step):
-            slot = (j + step) % NJ
-            copy(
-                in4.at[slot, whole],
-                in4.at[slot, whole],
-                send4.at[part, 0],
-                recv4.at[part, slot],
-                device(z, slot, x),
-            ).wait_recv()
-            place(slot, lambda one: in4[slot, one], range(begin, end))
-
-    scores = logits[...] + jnp.concatenate([shifts[:, 0, :], shifts[:, 1, :]], axis=1)
-    can = legal[pl.ds(depth, 1), :]
-    value = group_value(scores, can)
-    policy[...] = jnp.where(can > 0.0, scores - value, 0.0)
-    passed[...] = hand_down(value, owners[depth])
+        copy4(part).wait_recv()
+        for slot in range(begin, end):
+            place(in4, 1 - y_lo, slot)
+
+    scores[...] = logits[...] + jnp.concatenate([shifts[:, 0, :], shifts[:, 1, :]], axis=1)
+    own_legal[...] = jnp.broadcast_to(legal[pl.ds(depth, 1), :], (8, SL))
+    own_owner[...] = owners[depth]
 
     for i in range(NX):
         for other in range(1 if i == NX - 1 else 0, 2):
@@ -461,10 +443,24 @@
     for one in straight + onward + onward_down:
         one.wait_send()
 
-    @pl.loop(1, NJ)
-    def _(step):
-        for part in range(len(PARTS)):
-            copy4(step, part).wait_send()
+    for part in range(len(PARTS)):
+        copy4(part).wait_send()
+
+
+def last_pass(scores, legal, owner, policy_hbm, passed_hbm, policy, passed, stores):
+    can = legal[0:1, :]
+    copies = []
+    for i in range(CHUNKS):
+        rows = pl.ds(i * (HX // CHUNKS), HX // CHUNKS)
+        value = group_value(scores[rows, :], can)
+        policy[rows, :] = jnp.where(can > 0.0, scores[rows, :] - value, 0.0)
+        copies.append(pltpu.make_async_copy(policy.at[rows], policy_hbm.at[rows], stores.at[0, i]))
+        copies[-1].start()
+        passed[rows, :] = hand_down(value, owner[...])
+        copies.append(pltpu.make_async_copy(passed.at[rows], passed_hbm.at[rows], stores.at[1, i]))
+        copies[-1].start()
+    for one in copies:
+        one.wait()
 
 
 def local(reach, payoff, board_cards, hand_rank, logits, action_counts, parent_seq):
@@ -472,12 +468,16 @@
     vmem = pl.BlockSpec(memory_space=pltpu.VMEM)
     dma = pltpu.SemaphoreType.DMA
     f32, bf16, i16 = jnp.float32, jnp.bfloat16, jnp.int16
-    return pl.pallas_call(
+    scores, legal, owner = pl.pallas_call(
         kernel,
         name="prox",
-        out_shape=(jax.ShapeDtypeStruct((HX, SL), f32), jax.ShapeDtypeStruct((HX, SL), f32)),
+        out_shape=(
+            jax.ShapeDtypeStruct((HX, SL), f32),
+            jax.ShapeDtypeStruct((8, SL), f32),
+            jax.ShapeDtypeStruct((SL, SL), bf16),
+        ),
         in_specs=[pl.BlockSpec(memory_space=pl.ANY)] * 9,
-        out_specs=(vmem, vmem),
+        out_specs=(vmem, vmem, vmem),
         scratch_shapes=[
             pltpu.VMEM((NB * HX, SL), bf16),
             pltpu.VMEM((NB, 5), jnp.int32),
@@ -494,16 +494,17 @@
             pltpu.VMEM((NJ, HY, SL), i16),
             pltpu.VMEM((NZ, PAD, SL), i16),
             pltpu.VMEM((NZ - 1, PAD, SL), i16),
-            pltpu.VMEM((8, SX), f32),
-            pltpu.VMEM((8, SX), f32),
+            pltpu.VMEM((PAD, SX), f32),
+            pltpu.VMEM((PAD, SX), f32),
             pltpu.VMEM((SL, SX), bf16),
             pltpu.VMEM((HX, 2, 128), f32),
-            pltpu.VMEM((NL, HD, 2, 128), f32),
+            pltpu.VMEM((NL, HZ, 2, 128), f32),
             pltpu.VMEM((HY + 8, SL), f32),
             pltpu.VMEM((HZ, 8, 128), f32),
-            pltpu.VMEM((NL, HD, 8, 128), f32),
-            pltpu.VMEM((NZ, NL, HD, 2, 128), f32),
-            pltpu.VMEM((NJ, NZ, HD, 2, 128), f32),
+            pltpu.VMEM((NL, HZ, 8, 128), f32),
+            pltpu.VMEM((NL, HZ, 2, 128), f32),
+            pltpu.VMEM((NZ, HZ, 2, 128), f32),
+            pltpu.VMEM((NZ, HZ, 2, 128), f32),
             pltpu.VMEM((HX, 2, 128), f32),
             pltpu.VMEM((NL, SL), f32),
             pltpu.VMEM((NL, SL, SL), bf16),
@@ -513,8 +514,8 @@
             dma((NZ - 1,)),
             dma((NZ,)),
             dma((NZ,)),
-            dma((len(PARTS), NJ)),
-            dma((len(PARTS), NJ)),
+            dma((len(PARTS),)),
+            dma((len(PARTS),)),
             dma((NL,)),
             dma((NL,)),
             dma((NL,)),
@@ -540,6 +541,16 @@
             )
         ]
     )
+    hbm = pl.BlockSpec(memory_space=pl.ANY)
+    return pl.pallas_call(
+        last_pass,
+        name="last_pass",
+        out_shape=(jax.ShapeDtypeStruct((HX, SL), f32), jax.ShapeDtypeStruct((HX, SL), f32)),
+        in_specs=[vmem] * 3,
+        out_specs=(hbm, hbm),
+        scratch_shapes=[pltpu.VMEM((HX, SL), f32), pltpu.VMEM((HX, SL), f32), dma((2, CHUNKS))],
+        compiler_params=pltpu.CompilerParams(vmem_limit_bytes=32 * 1024 * 1024),
+    )(scores, legal, owner)
 
 
 def solution(mesh):

time: 58.8 us -> 57.1 us (0.971); the launches traced: 58.7 us -> 56.1 us
  local copies, waits for them, and re-layouts: 1.49 us -> 0 us
  Pallas kernels: 56.5 us -> 55.5 us
    pallas_call x1, Pallas kernels: 56.5 us -> 53.2 us  [local(): pl.pallas_call(kernel, name='prox', out_shape=(jax.ShapeDtypeStruct((HX,...]
    pallas_call x0 -> x1, Pallas kernels: none -> 2.24 us  [local(): pl.pallas_call(last_pass, name='last_pass', out_shape=(jax.ShapeDtypeStru...]
    unnamed x2 -> x0, local copies, waits for them, and re-layouts: 1.49 us -> none
where the time goes in v5:
time: 57.1 us; the launch traced here: 56.1 us
  Pallas kernels  55.5 us (97%)
  between operations  0.64 us (1%)
    pallas_call x1, Pallas kernels, local(): pl.pallas_call(kernel, name='prox', out_shape=(jax.ShapeDtypeStruct((HX,...  53.2 us
    pallas_call x1, Pallas kernels, local(): pl.pallas_call(last_pass, name='last_pass', out_shape=(jax.ShapeDtypeStru...  2.24 us

profile of v5, /device:TPU:1, one launch (start us, length us, event | category | flops | bytes accessed | tf_op | source)
XLA Modules:
  0.0 56.1 jit_solution(2850687155542455628)
XLA Ops:
  0.6 53.2 %prox.1 = (f32[384,256]{1,0:T(8,128)S(1)}, f32[8,256]{1,0:T(8,128)S(1)}, bf16[256,256]{1,0:T(8,128)(2,1)S(1)}) custom-call(bf16[3072,256]{1,0:T(8,128)(2,1)} %bitcast.1, bf16[256,1024]{1,0:T(8,128)(2,1)} %payoff.1, s32[8,5]{1,0:T(8,128)} %cards_hbm.1, s32[8,1326]{1,0:T(8,128)} %rank_hbm.1, f32[384,256]{1,0:T(8,128)} %logits_hbm.1, s32[4,64]{1,0:T(4,128)} %counts_hbm.1, ...), custom_call_target="tpu_custom_call" | custom-call | tf_op jit(solution)/shard_map/prox/pallas_call | solution.py:471
  53.9 2.2 %last_pass.1 = (f32[384,256]{1,0:T(8,128)}, f32[384,256]{1,0:T(8,128)}) custom-call(f32[384,256]{1,0:T(8,128)S(1)} %get-tuple-element.5.scores, f32[8,256]{1,0:T(8,128)S(1)} %get-tuple-element.6.legal, bf16[256,256]{1,0:T(8,128)(2,1)S(1)} %get-tuple-element.7.owner), custom_call_target="tpu_custom_call" | custom-call | tf_op jit(solution)/shard_map/last_pass/pallas_call | solution.py:545

commit v6 on v5

--- a/solution.py
+++ b/solution.py
@@ -36,7 +36,7 @@
 PLACES = (0, 1, -1, 2, -2, 5, -5, -3, -4, -6, -7, 3, 4, 6, 7, 8)
 PARTS = ((0, 7), (7, 11), (11, 16))
 ROW_PEERS = 2 * NX - 1
-CHUNKS = 3
+CHUNKS = 2
 NAN = float("nan")
 
 
@@ -93,6 +93,8 @@
     table_hbm,
     onehot_hbm,
     scores,
+    own_policy,
+    own_passed,
     own_legal,
     own_owner,
     reach,
@@ -116,6 +118,7 @@
     logit_tiles,
     logit_rows,
     total2,
+    halves,
     out5,
     in5,
     out3,
@@ -156,21 +159,23 @@
             src_ref=src, dst_ref=dst, send_sem=send, recv_sem=recv, device_id=to, device_id_type=MESH
         )
 
+    def loaded(i, src, dst):
+        return pltpu.make_async_copy(src, dst, load.at[i])
+
     loads = [
-        pltpu.make_async_copy(src, dst, load.at[i])
-        for i, (src, dst) in enumerate(
-            [
-                (rank_hbm, rank),
-                (cards_hbm, cards),
-                (table_hbm, table),
-                (onehot_hbm, onehot),
-                (reach_hbm, reach),
-                (payoff, pay),
-                (logits_hbm, logits),
-                (counts_hbm, counts),
-                (parents_hbm, parents),
-            ]
-        )
+        loaded(0, rank_hbm, rank),
+        loaded(1, cards_hbm, cards),
+        loaded(2, table_hbm, table),
+        loaded(3, onehot_hbm, onehot),
+    ]
+    for b in range(NB):
+        rows = pl.ds(b * HX, HX)
+        loads.append(loaded(4 + b, reach_hbm.at[rows], reach.at[rows]))
+    later = [
+        loaded(4 + NB, logits_hbm, logits),
+        loaded(5 + NB, counts_hbm, counts),
+        loaded(6 + NB, parents_hbm, parents),
+        loaded(7 + NB, payoff, pay),
     ]
     for one in loads:
         one.start()
@@ -205,8 +210,10 @@
 
     own = pl.ds(pl.multiple_of(x * HX, HX), HX)
 
-    loads[3].wait()
-    loads[4].wait()
+    for one in loads[3:]:
+        one.wait()
+    for one in later:
+        one.start()
 
     def partial(to_x):
         rows = pl.ds(pl.multiple_of(to_x * HX, HX), HX)
@@ -264,7 +271,7 @@
         pl.semaphore_signal(know.at[1], inc=1, device_id=device(along(dz), j, x), device_id_type=MESH)
     in1[me1] = out1[x, y_lo]
 
-    for one in loads[5:]:
+    for one in later:
         one.wait()
 
     for half in range(2):
@@ -311,10 +318,10 @@
             in1.at[slot], in1.at[slot], send1.at[0, 0], recv1.at[slot], device(z, j, (x + 1) % NX)
         ).wait_recv()
         total += in1[slot].astype(jnp.int32)
-    total2[:HY, :] = total.astype(jnp.float32) * (SCALE_PLANE / SCALE)
-    total2[HY:, :] = jnp.zeros((8, SL), jnp.float32)
+    total2[...] = total.astype(jnp.float32) * (SCALE_PLANE / SCALE)
     for to_z in range(NZ):
-        rows = jnp.round(total2[to_z * HZ : to_z * HZ + PAD, :])
+        rows = total2[to_z * HZ : (to_z + 1) * HZ, :]
+        rows = jnp.round(jnp.concatenate([rows[:, :128], rows[:, 128:]], axis=0))
         out2[to_z] = rows.astype(jnp.int32).astype(jnp.int16)
 
     pl.semaphore_wait(know.at[1], 2)
@@ -342,7 +349,9 @@
     for i in range(NZ - 2, -1, -1):
         copy2(i).wait_recv()
         total += in2[i].astype(jnp.int32)
-    counter = total.astype(jnp.float32)
+    halves[0 : 2 * HZ, :] = total.astype(jnp.float32)
+    halves[2 * HZ :, :] = jnp.zeros((8, 128), jnp.float32)
+    counter = jnp.concatenate([halves[0:PAD, :], halves[HZ : HZ + PAD, :]], axis=1)
     high = counter.astype(jnp.bfloat16).astype(jnp.float32)
     both = jnp.concatenate([high, counter - high], axis=0).astype(jnp.bfloat16)
     partial_gradient = jnp.dot(both, pay[...], preferred_element_type=jnp.float32)
@@ -423,14 +432,24 @@
         copy4(part).start()
         for slot in range(begin, end):
             place(in3, y_lo, slot)
+    def half_scores(half):
+        rows = pl.ds(half * HY, HY)
+        here = logits[pl.ds(pl.multiple_of(half * HY, HY), HY), :]
+        return here + jnp.concatenate([shifts[rows, 0, :], shifts[rows, 1, :]], axis=1)
+
+    can = legal[pl.ds(depth, 1), :]
+    own_legal[...] = jnp.broadcast_to(can, (8, SL))
+    own_owner[...] = owners[depth]
+    here = half_scores(y_lo)
+    value = group_value(here, can)
+    own_policy[...] = jnp.where(can > 0.0, here - value, 0.0)
+    own_passed[...] = hand_down(value, owners[depth])
+
     for part, (begin, end) in enumerate(PARTS):
         copy4(part).wait_recv()
         for slot in range(begin, end):
             place(in4, 1 - y_lo, slot)
-
-    scores[...] = logits[...] + jnp.concatenate([shifts[:, 0, :], shifts[:, 1, :]], axis=1)
-    own_legal[...] = jnp.broadcast_to(legal[pl.ds(depth, 1), :], (8, SL))
-    own_owner[...] = owners[depth]
+    scores[...] = half_scores(1 - y_lo)
 
     for i in range(NX):
         for other in range(1 if i == NX - 1 else 0, 2):
@@ -447,18 +466,28 @@
         copy4(part).wait_send()
 
 
-def last_pass(scores, legal, owner, policy_hbm, passed_hbm, policy, passed, stores):
+def last_pass(scores, own_policy, own_passed, legal, owner, policy_hbm, passed_hbm, policy, passed, stores):
+    y_lo = lax.axis_index("board") % 2
+
+    def store(src, dst, half, first, count, sem):
+        rows = pl.ds(pl.multiple_of(half * HY + first, 8), count)
+        one = pltpu.make_async_copy(src.at[pl.ds(first, count)], dst.at[rows], sem)
+        one.start()
+        return one
+
+    copies = [
+        store(own_policy, policy_hbm, y_lo, 0, HY, stores.at[0, CHUNKS]),
+        store(own_passed, passed_hbm, y_lo, 0, HY, stores.at[1, CHUNKS]),
+    ]
     can = legal[0:1, :]
-    copies = []
+    count = HY // CHUNKS
     for i in range(CHUNKS):
-        rows = pl.ds(i * (HX // CHUNKS), HX // CHUNKS)
+        rows = pl.ds(i * count, count)
         value = group_value(scores[rows, :], can)
         policy[rows, :] = jnp.where(can > 0.0, scores[rows, :] - value, 0.0)
-        copies.append(pltpu.make_async_copy(policy.at[rows], policy_hbm.at[rows], stores.at[0, i]))
-        copies[-1].start()
+        copies.append(store(policy, policy_hbm, 1 - y_lo, i * count, count, stores.at[0, i]))
         passed[rows, :] = hand_down(value, owner[...])
-        copies.append(pltpu.make_async_copy(passed.at[rows], passed_hbm.at[rows], stores.at[1, i]))
-        copies[-1].start()
+        copies.append(store(passed, passed_hbm, 1 - y_lo, i * count, count, stores.at[1, i]))
     for one in copies:
         one.wait()
 
@@ -468,16 +497,18 @@
     vmem = pl.BlockSpec(memory_space=pltpu.VMEM)
     dma = pltpu.SemaphoreType.DMA
     f32, bf16, i16 = jnp.float32, jnp.bfloat16, jnp.int16
-    scores, legal, owner = pl.pallas_call(
+    rest = pl.pallas_call(
         kernel,
         name="prox",
         out_shape=(
-            jax.ShapeDtypeStruct((HX, SL), f32),
+            jax.ShapeDtypeStruct((HY, SL), f32),
+            jax.ShapeDtypeStruct((HY, SL), f32),
+            jax.ShapeDtypeStruct((HY, SL), f32),
             jax.ShapeDtypeStruct((8, SL), f32),
             jax.ShapeDtypeStruct((SL, SL), bf16),
         ),
         in_specs=[pl.BlockSpec(memory_space=pl.ANY)] * 9,
-        out_specs=(vmem, vmem, vmem),
+        out_specs=(vmem,) * 5,
         scratch_shapes=[
             pltpu.VMEM((NB * HX, SL), bf16),
             pltpu.VMEM((NB, 5), jnp.int32),
@@ -487,19 +518,20 @@
             pltpu.VMEM((NL, SL // ACT), jnp.int32),
             pltpu.VMEM((8, HP), f32),
             pltpu.VMEM((HP, 128), bf16),
-            dma((9,)),
+            dma((NB + 8,)),
             pltpu.VMEM((NB, HP), f32),
             pltpu.VMEM((HP, NB), f32),
             pltpu.VMEM((NX, 2, HY, SL), i16),
             pltpu.VMEM((NJ, HY, SL), i16),
-            pltpu.VMEM((NZ, PAD, SL), i16),
-            pltpu.VMEM((NZ - 1, PAD, SL), i16),
+            pltpu.VMEM((NZ, 2 * HZ, 128), i16),
+            pltpu.VMEM((NZ - 1, 2 * HZ, 128), i16),
             pltpu.VMEM((PAD, SX), f32),
             pltpu.VMEM((PAD, SX), f32),
             pltpu.VMEM((SL, SX), bf16),
             pltpu.VMEM((HX, 2, 128), f32),
             pltpu.VMEM((NL, HZ, 2, 128), f32),
-            pltpu.VMEM((HY + 8, SL), f32),
+            pltpu.VMEM((HY, SL), f32),
+            pltpu.VMEM((2 * HZ + 8, 128), f32),
             pltpu.VMEM((HZ, 8, 128), f32),
             pltpu.VMEM((NL, HZ, 8, 128), f32),
             pltpu.VMEM((NL, HZ, 2, 128), f32),
@@ -546,11 +578,11 @@
         last_pass,
         name="last_pass",
         out_shape=(jax.ShapeDtypeStruct((HX, SL), f32), jax.ShapeDtypeStruct((HX, SL), f32)),
-        in_specs=[vmem] * 3,
+        in_specs=[vmem] * 5,
         out_specs=(hbm, hbm),
-        scratch_shapes=[pltpu.VMEM((HX, SL), f32), pltpu.VMEM((HX, SL), f32), dma((2, CHUNKS))],
+        scratch_shapes=[pltpu.VMEM((HY, SL), f32), pltpu.VMEM((HY, SL), f32), dma((2, CHUNKS + 1))],
         compiler_params=pltpu.CompilerParams(vmem_limit_bytes=32 * 1024 * 1024),
-    )(scores, legal, owner)
+    )(*rest)
 
 
 def solution(mesh):

time: 57.1 us -> 55.4 us (0.970)
  the two profiles are of different devices: /device:TPU:1 before, /device:TPU:8 now
where the time goes in v6:
time: 55.4 us; the launch traced here: 55.2 us
  Pallas kernels  54.6 us (99%)
  between operations  0.64 us (1%)
    pallas_call x1, Pallas kernels, local(): pl.pallas_call(kernel, name='prox', out_shape=(jax.ShapeDtypeStruct((HY,...  53.1 us
    pallas_call x1, Pallas kernels, local(): pl.pallas_call(last_pass, name='last_pass', out_shape=(jax.ShapeDtypeStru...  1.49 us

profile of v6, /device:TPU:8, one launch (start us, length us, event | category | flops | bytes accessed | tf_op | source)
XLA Modules:
  0.0 55.2 jit_solution(10486410940840575500)
XLA Ops:
  0.6 53.1 %prox.1 = (f32[192,256]{1,0:T(8,128)S(1)}, f32[192,256]{1,0:T(8,128)S(1)}, f32[192,256]{1,0:T(8,128)S(1)}, f32[8,256]{1,0:T(8,128)S(1)}, bf16[256,256]{1,0:T(8,128)(2,1)S(1)}) custom-call(bf16[3072,256]{1,0:T(8,128)(2,1)} %bitcast.1, bf16[256,1024]{1,0:T(8,128)(2,1)} %payoff.1, s32[8,5]{1,0:T(8,128)} %cards_hbm.1, s32[8,1326]{1,0:T(8,128)} %rank_hbm.1, ...), custom_call_target="tpu_custom_call" | custom-call | tf_op jit(solution)/shard_map/prox/pallas_call | solution.py:500
  53.7 1.5 %last_pass.1 = (f32[384,256]{1,0:T(8,128)}, f32[384,256]{1,0:T(8,128)}) custom-call(f32[192,256]{1,0:T(8,128)S(1)} %get-tuple-element.7.scores, f32[192,256]{1,0:T(8,128)S(1)} %get-tuple-element.8.own_policy, f32[192,256]{1,0:T(8,128)S(1)} %get-tuple-element.9.own_passed, f32[8,256]{1,0:T(8,128)S(1)} %get-tuple-element.10.legal, ...), custom_call_target="tpu_custom_call" | custom-call | tf_op jit(solution)/shard_map/last_pass/pallas_call | solution.py:577

commit v7 on v6

--- a/solution.py
+++ b/solution.py
@@ -12,17 +12,17 @@
 NZ = 16
 NX = 4
 NL = 4
-NJ = 8
 HX = 384
 HP = NX * HX
 HY = HX // 2
+HH = HY // 2
 HZ = HY // NZ
 PAD = 16
 SL = 256
 SX = NL * SL
 NB = 8
-BOUND = float(NB * HX)
-SCALE = 32767.0 / BOUND
+BOUND = float(2 * NB * HX)
+SCALE = 32700.0 / BOUND
 LIVE = 45 * 44 // 2
 BOUND_PLANE = float(2 * NB * LIVE)
 SCALE_PLANE = 32700.0 / BOUND_PLANE
@@ -35,7 +35,7 @@
 GREET = (1, -1, 2, -2)
 PLACES = (0, 1, -1, 2, -2, 5, -5, -3, -4, -6, -7, 3, 4, 6, 7, 8)
 PARTS = ((0, 7), (7, 11), (11, 16))
-ROW_PEERS = 2 * NX - 1
+ROW_PEERS = 5
 CHUNKS = 2
 NAN = float("nan")
 
@@ -109,7 +109,9 @@
     ranks,
     ranks_t,
     out1,
-    in1,
+    relay,
+    in_x,
+    in_y,
     out2,
     in2,
     rows16,
@@ -129,6 +131,8 @@
     owners,
     send1,
     recv1,
+    send_r,
+    recv_r,
     send2,
     recv2,
     send3,
@@ -184,10 +188,12 @@
         return (x + 2 + i + i * (i - 1) // 2) % NX
 
     barrier = pltpu.get_barrier_semaphore()
-    for i in range(NX):
-        for other in range(1 if i == NX - 1 else 0, 2):
+    for i in (1, 2):
+        for other in range(2):
             to_j = (y_lo + other) % 2 * NL + depth
             pl.semaphore_signal(barrier, inc=1, device_id=device(z, to_j, hop_x(i)), device_id_type=MESH)
+    to_j = (1 - y_lo) * NL + depth
+    pl.semaphore_signal(barrier, inc=1, device_id=device(z, to_j, x), device_id_type=MESH)
     for step in range(1, NL):
         to_j = y_lo * NL + (depth + step) % NL
         pl.semaphore_signal(barrier, inc=1, device_id=device(z, to_j, x), device_id_type=MESH)
@@ -235,17 +241,31 @@
             )
         return jnp.round(total * SCALE).astype(jnp.int32).astype(jnp.int16)
 
-    me1 = x * 2 + y_lo
-
-    def copy1(i, other):
-        to_x, to_y = hop_x(i), (y_lo + other) % 2
+    def half_rows(part):
+        return pl.ds(part * HH, HH)
+
+    def copy_r(part):
         return copy(
-            out1.at[to_x, to_y],
-            in1.at[me1],
-            send1.at[i, other],
-            recv1.at[me1],
+            out1.at[hop_x(0), pl.ds(0, 2), half_rows(part)],
+            relay.at[part],
+            send_r.at[part],
+            recv_r.at[part],
+            device(z, j, hop_x(2 - part)),
+        )
+
+    def copy1(i, other, part):
+        to_x, to_y, way = hop_x(i), (y_lo + other) % 2, 2 - i
+        return copy(
+            out1.at[to_x, to_y, half_rows(part)],
+            in_x.at[way, y_lo, half_rows(part)],
+            send1.at[way, other, part],
+            recv1.at[way, y_lo, part],
             device(z, to_y * NL + depth, to_x),
         )
+
+    copy_y = copy(
+        out1.at[x, 1 - y_lo], in_y, send_r.at[2], recv_r.at[2], device(z, (1 - y_lo) * NL + depth, x)
+    )
 
     @pl.loop(0, NX)
     def _(i):
@@ -259,18 +279,32 @@
                 pl.semaphore_signal(
                     know.at[0], inc=1, device_id=device(along(dz), j, x), device_id_type=MESH
                 )
-
-        copy1(i, 1).start()
-
-        @pl.when(i < NX - 1)
+            copy_r(0).start()
+            copy_r(1).start()
+
+        @pl.when(i == 1)
         def _():
-            copy1(i, 0).start()
+            copy1(1, 1, 0).start()
+            copy1(1, 0, 0).start()
+
+        @pl.when(i == 2)
+        def _():
+            copy1(2, 1, 1).start()
+            copy1(2, 0, 1).start()
+
+    copy_y.start()
+    for i, part in ((1, 1), (2, 0)):
+        copy_r(part).wait_recv()
+        to_x = hop_x(i)
+        both_rows = slice(part * HH, part * HH + HH)
+        here = out1[to_x, :, both_rows, :].astype(jnp.int32)
+        out1[to_x, :, both_rows, :] = (here + relay[part].astype(jnp.int32)).astype(jnp.int16)
+        copy1(i, 1, part).start()
+        copy1(i, 0, part).start()
 
     pl.semaphore_wait(know.at[0], 2)
     for dz in (4, -4):
         pl.semaphore_signal(know.at[1], inc=1, device_id=device(along(dz), j, x), device_id_type=MESH)
-    in1[me1] = out1[x, y_lo]
-
     for one in later:
         one.wait()
 
@@ -311,13 +345,16 @@
     for level in range(NL):
         owners[level] = jnp.where(seq == parents_wide[level : level + 1, :], 1.0, 0.0).astype(jnp.bfloat16)
 
-    total = in1[me1].astype(jnp.int32)
-    for i in range(ROW_PEERS):
-        slot = (me1 + 1 + i) % NJ
-        copy(
-            in1.at[slot], in1.at[slot], send1.at[0, 0], recv1.at[slot], device(z, j, (x + 1) % NX)
-        ).wait_recv()
-        total += in1[slot].astype(jnp.int32)
+    total = out1[x, y_lo].astype(jnp.int32)
+    copy_y.wait_recv()
+    total += in_y[...].astype(jnp.int32)
+    for way in range(2):
+        for from_y in range(2):
+            for part in range(2):
+                rows = in_x.at[way, from_y, half_rows(part)]
+                sem = recv1.at[way, from_y, part]
+                copy(rows, rows, send1.at[0, 0, 0], sem, device(z, j, hop_x(1))).wait_recv()
+            total += in_x[way, from_y].astype(jnp.int32)
     total2[...] = total.astype(jnp.float32) * (SCALE_PLANE / SCALE)
     for to_z in range(NZ):
         rows = total2[to_z * HZ : (to_z + 1) * HZ, :]
@@ -451,9 +488,12 @@
             place(in4, 1 - y_lo, slot)
     scores[...] = half_scores(1 - y_lo)
 
-    for i in range(NX):
-        for other in range(1 if i == NX - 1 else 0, 2):
-            copy1(i, other).wait_send()
+    for part in range(2):
+        copy_r(part).wait_send()
+        for other in range(2):
+            copy1(1, other, part).wait_send()
+            copy1(2, other, part).wait_send()
+    copy_y.wait_send()
     for i in range(NZ - 1):
         copy2(i).wait_send()
     for step in range(1, NL):
@@ -522,7 +562,9 @@
             pltpu.VMEM((NB, HP), f32),
             pltpu.VMEM((HP, NB), f32),
             pltpu.VMEM((NX, 2, HY, SL), i16),
-            pltpu.VMEM((NJ, HY, SL), i16),
+            pltpu.VMEM((2, 2, HH, SL), i16),
+            pltpu.VMEM((2, 2, HY, SL), i16),
+            pltpu.VMEM((HY, SL), i16),
             pltpu.VMEM((NZ, 2 * HZ, 128), i16),
             pltpu.VMEM((NZ - 1, 2 * HZ, 128), i16),
             pltpu.VMEM((PAD, SX), f32),
@@ -540,8 +582,10 @@
             pltpu.VMEM((HX, 2, 128), f32),
             pltpu.VMEM((NL, SL), f32),
             pltpu.VMEM((NL, SL, SL), bf16),
-            dma((NX, 2)),
-            dma((NJ,)),
+            dma((2, 2, 2)),
+            dma((2, 2, 2)),
+            dma((3,)),
+            dma((3,)),
             dma((NZ - 1,)),
             dma((NZ - 1,)),
             dma((NZ,)),

time: 55.4 us -> 54.1 us (0.977)
  Pallas kernels: 54.6 us -> 53.3 us
    pallas_call x1, Pallas kernels: 53.1 us -> 51.8 us  [local(): pl.pallas_call(kernel, name='prox', out_shape=(jax.ShapeDtypeStruct((HY,...]
where the time goes in v7:
time: 54.1 us; the launch traced here: 53.9 us
  Pallas kernels  53.3 us (99%)
  between operations  0.64 us (1%)
    pallas_call x1, Pallas kernels, local(): pl.pallas_call(kernel, name='prox', out_shape=(jax.ShapeDtypeStruct((HY,...  51.8 us
    pallas_call x1, Pallas kernels, local(): pl.pallas_call(last_pass, name='last_pass', out_shape=(jax.ShapeDtypeStru...  1.49 us

profile of v7, /device:TPU:8, one launch (start us, length us, event | category | flops | bytes accessed | tf_op | source)
XLA Modules:
  0.0 53.9 jit_solution(5839663912826768453)
XLA Ops:
  0.6 51.8 %prox.1 = (f32[192,256]{1,0:T(8,128)S(1)}, f32[192,256]{1,0:T(8,128)S(1)}, f32[192,256]{1,0:T(8,128)S(1)}, f32[8,256]{1,0:T(8,128)S(1)}, bf16[256,256]{1,0:T(8,128)(2,1)S(1)}) custom-call(bf16[3072,256]{1,0:T(8,128)(2,1)} %bitcast.1, bf16[256,1024]{1,0:T(8,128)(2,1)} %payoff.1, s32[8,5]{1,0:T(8,128)} %cards_hbm.1, s32[8,1326]{1,0:T(8,128)} %rank_hbm.1, ...), custom_call_target="tpu_custom_call" | custom-call | tf_op jit(solution)/shard_map/prox/pallas_call | solution.py:540
  52.4 1.5 %last_pass.1 = (f32[384,256]{1,0:T(8,128)}, f32[384,256]{1,0:T(8,128)}) custom-call(f32[192,256]{1,0:T(8,128)S(1)} %get-tuple-element.7.scores, f32[192,256]{1,0:T(8,128)S(1)} %get-tuple-element.8.own_policy, f32[192,256]{1,0:T(8,128)S(1)} %get-tuple-element.9.own_passed, f32[8,256]{1,0:T(8,128)S(1)} %get-tuple-element.10.legal, ...), custom_call_target="tpu_custom_call" | custom-call | tf_op jit(solution)/shard_map/last_pass/pallas_call | solution.py:621

commit v8 on v7

--- a/solution.py
+++ b/solution.py
@@ -71,6 +71,18 @@
         top = group_reduce(masked, jnp.maximum)
         total = group_reduce(jnp.exp(masked - top), jnp.add)
         parts.append(top + jnp.log(total))
+    return jnp.concatenate(parts, axis=1)
+
+
+def first_value(scores, legal):
+    parts = []
+    for half in range(2):
+        cols = slice(half * 128, half * 128 + 128)
+        slots = [jnp.where(legal[:, cols] > 0.0, scores[:, cols], -jnp.inf)]
+        slots += [pltpu.roll(slots[0], 128 - step, 1) for step in range(1, ACT)]
+        top = jnp.maximum(jnp.maximum(slots[0], slots[1]), jnp.maximum(slots[2], slots[3]))
+        terms = [jnp.exp(slot - top) for slot in slots]
+        parts.append(top + jnp.log((terms[0] + terms[1]) + (terms[2] + terms[3])))
     return jnp.concatenate(parts, axis=1)
 
 
@@ -211,7 +223,14 @@
     for card in range(5):
         one = cards[:, card : card + 1].astype(jnp.float32)
         hit = hit | (first == one) | (second == one)
-    ranks[...] = jnp.where(hit, NAN, ranks[...])
+    left = ranks[...]
+    exponent = jnp.floor(left * (1.0 / 128.0))
+    ordered = (1.0 + (left - exponent * 128.0) * (1.0 / 128.0)) * 2.0**-29
+    for bit in range(6):
+        rest = jnp.floor(exponent * 0.5)
+        ordered = jnp.where(exponent - 2.0 * rest > 0.5, ordered * 2.0 ** (1 << bit), ordered)
+        exponent = rest
+    ranks[...] = jnp.where(hit, NAN, ordered)
     ranks_t[...] = ranks[...].T
 
     own = pl.ds(pl.multiple_of(x * HX, HX), HX)
@@ -224,16 +243,16 @@
     def partial(to_x):
         rows = pl.ds(pl.multiple_of(to_x * HX, HX), HX)
         shared = dot_t(onehot[rows, :], onehot[own, :])
-        apart = jnp.where(shared > 0.0, 0.0, 1.0)
+        apart = jnp.where(shared > 0.0, 0.0, 1.0).astype(jnp.bfloat16)
         minus = -apart
+        zero = jnp.zeros((HX, HX), jnp.bfloat16)
         total = jnp.zeros((HX, SL), jnp.float32)
         for pair in range(NB // 2):
             sides = []
             for b in (2 * pair, 2 * pair + 1):
-                mine = ranks_t[rows, b : b + 1]
-                theirs = ranks[b : b + 1, own]
-                sign = jnp.where(theirs < mine, apart, jnp.where(theirs > mine, minus, 0.0))
-                sides.append(sign.astype(jnp.bfloat16))
+                mine = jnp.broadcast_to(ranks_t[rows, b : b + 1].astype(jnp.bfloat16), (HX, HX))
+                theirs = jnp.broadcast_to(ranks[b : b + 1, own].astype(jnp.bfloat16), (HX, HX))
+                sides.append(jnp.where(theirs < mine, apart, jnp.where(theirs > mine, minus, zero)))
             total += jnp.dot(
                 jnp.concatenate(sides, axis=1),
                 reach[2 * HX * pair : 2 * HX * (pair + 1), :],
@@ -423,7 +442,7 @@
         out3[level, :, 0, :] = shift[:HZ, :128]
         out3[level, :, 1, :] = shift[:HZ, 128:]
         if level:
-            value = group_value(logit16[:, cols] + shift, legal[level : level + 1, :])
+            value = first_value(logit16[:, cols] + shift, legal[level : level + 1, :])
             incoming = hand_down(value, owners[level])
 
     in3[0] = out3[depth]

time: 54.1 us -> 53.1 us (0.982)
  the two profiles are of different devices: /device:TPU:8 before, /device:TPU:10 now
where the time goes in v8:
time: 53.1 us; the launch traced here: 53 us
  Pallas kernels  52.3 us (98%)
  between operations  0.64 us (1%)
    pallas_call x1, Pallas kernels, local(): pl.pallas_call(kernel, name='prox', out_shape=(jax.ShapeDtypeStruct((HY,...  50.8 us
    pallas_call x1, Pallas kernels, local(): pl.pallas_call(last_pass, name='last_pass', out_shape=(jax.ShapeDtypeStru...  1.49 us

profile of v8, /device:TPU:10, one launch (start us, length us, event | category | flops | bytes accessed | tf_op | source)
XLA Modules:
  0.0 53.0 jit_solution(12182057590010544859)
XLA Ops:
  0.6 50.8 %prox.1 = (f32[192,256]{1,0:T(8,128)S(1)}, f32[192,256]{1,0:T(8,128)S(1)}, f32[192,256]{1,0:T(8,128)S(1)}, f32[8,256]{1,0:T(8,128)S(1)}, bf16[256,256]{1,0:T(8,128)(2,1)S(1)}) custom-call(bf16[3072,256]{1,0:T(8,128)(2,1)} %bitcast.1, bf16[256,1024]{1,0:T(8,128)(2,1)} %payoff.1, s32[8,5]{1,0:T(8,128)} %cards_hbm.1, s32[8,1326]{1,0:T(8,128)} %rank_hbm.1, ...), custom_call_target="tpu_custom_call" | custom-call | tf_op jit(solution)/shard_map/prox/pallas_call | solution.py:559
  51.5 1.5 %last_pass.1 = (f32[384,256]{1,0:T(8,128)}, f32[384,256]{1,0:T(8,128)}) custom-call(f32[192,256]{1,0:T(8,128)S(1)} %get-tuple-element.7.scores, f32[192,256]{1,0:T(8,128)S(1)} %get-tuple-element.8.own_policy, f32[192,256]{1,0:T(8,128)S(1)} %get-tuple-element.9.own_passed, f32[8,256]{1,0:T(8,128)S(1)} %get-tuple-element.10.legal, ...), custom_call_target="tpu_custom_call" | custom-call | tf_op jit(solution)/shard_map/last_pass/pallas_call | solution.py:640

commit v9 on v8

--- a/solution.py
+++ b/solution.py
@@ -91,7 +91,10 @@
     rest = value - a.astype(jnp.float32)
     b = rest.astype(jnp.bfloat16)
     c = (rest - b.astype(jnp.float32)).astype(jnp.bfloat16)
-    return dot_t(a, owner_t) + dot_t(b, owner_t) + dot_t(c, owner_t)
+    if value.shape[0] > 2 * PAD:
+        return dot_t(a, owner_t) + dot_t(b, owner_t) + dot_t(c, owner_t)
+    all_parts = dot_t(jnp.concatenate([a, b, c], axis=0), owner_t)
+    return all_parts[:PAD] + all_parts[PAD : 2 * PAD] + all_parts[2 * PAD :]
 
 
 def kernel(
@@ -364,17 +367,23 @@
     for level in range(NL):
         owners[level] = jnp.where(seq == parents_wide[level : level + 1, :], 1.0, 0.0).astype(jnp.bfloat16)
 
-    total = out1[x, y_lo].astype(jnp.int32)
+    def plane_rows(way, from_y, part):
+        rows = in_x.at[way, from_y, half_rows(part)]
+        sem = recv1.at[way, from_y, part]
+        copy(rows, rows, send1.at[0, 0, 0], sem, device(z, j, hop_x(1))).wait_recv()
+        return in_x[way, from_y, part * HH : part * HH + HH, :].astype(jnp.int32)
+
     copy_y.wait_recv()
-    total += in_y[...].astype(jnp.int32)
-    for way in range(2):
-        for from_y in range(2):
-            for part in range(2):
-                rows = in_x.at[way, from_y, half_rows(part)]
-                sem = recv1.at[way, from_y, part]
-                copy(rows, rows, send1.at[0, 0, 0], sem, device(z, j, hop_x(1))).wait_recv()
-            total += in_x[way, from_y].astype(jnp.int32)
-    total2[...] = total.astype(jnp.float32) * (SCALE_PLANE / SCALE)
+    sums = []
+    for part in range(2):
+        rows = slice(part * HH, part * HH + HH)
+        sums.append(out1[x, y_lo, rows, :].astype(jnp.int32) + in_y[rows, :].astype(jnp.int32))
+    for late in range(2):
+        for part in range(2):
+            for from_y in range(2):
+                sums[part] += plane_rows(1 - part if late == 0 else part, from_y, part)
+    for part in range(2):
+        total2[part * HH : part * HH + HH, :] = sums[part].astype(jnp.float32) * (SCALE_PLANE / SCALE)
     for to_z in range(NZ):
         rows = total2[to_z * HZ : (to_z + 1) * HZ, :]
         rows = jnp.round(jnp.concatenate([rows[:, :128], rows[:, 128:]], axis=0))
@@ -410,35 +419,37 @@
     counter = jnp.concatenate([halves[0:PAD, :], halves[HZ : HZ + PAD, :]], axis=1)
     high = counter.astype(jnp.bfloat16).astype(jnp.float32)
     both = jnp.concatenate([high, counter - high], axis=0).astype(jnp.bfloat16)
-    partial_gradient = jnp.dot(both, pay[...], preferred_element_type=jnp.float32)
-    partial_gradient = (partial_gradient[:PAD] + partial_gradient[PAD:]) * (1.0 / SCALE_PLANE)
-    for group in range(8):
-        out5[:, group, :] = partial_gradient[:HZ, group * 128 : (group + 1) * 128]
-
-    def copy5(step):
-        to = depth_peer(step)
+
+    def copy5(pair, step):
         return copy(
-            out5,
-            in5.at[step],
-            send5.at[step],
-            recv5.at[step],
-            device(z, y_lo * NL + to, x),
+            out5.at[pair],
+            in5.at[step, pair],
+            send5.at[pair, step],
+            recv5.at[pair, step],
+            device(z, y_lo * NL + depth_peer(step), x),
         )
 
-    for step in (2, 1, 3):
-        copy5(step).start()
-    for step in range(1, NL):
-        copy5(step).wait_recv()
-    total = out5[...] + in5[1] + in5[2] + in5[3]
-    in5[0] = total
-    for group in range(8):
-        rows16[0:HZ, group * 128 : (group + 1) * 128] = in5[0, :, group, :]
-    gradient = rows16[...]
+    for pair in (1, 0):
+        cols = slice(pair * 2 * SL, (pair + 1) * 2 * SL)
+        part = jnp.dot(both, pay[:, cols], preferred_element_type=jnp.float32)
+        part = (part[:PAD] + part[PAD:]) * (1.0 / SCALE_PLANE)
+        for group in range(4):
+            out5[pair, :, group, :] = part[:HZ, group * 128 : (group + 1) * 128]
+        for step in (2, 1, 3):
+            copy5(pair, step).start()
 
     incoming = jnp.zeros((PAD, SL), jnp.float32)
     for level in range(NL - 1, -1, -1):
         cols = slice(level * SL, (level + 1) * SL)
-        shift = gradient[:, cols] + incoming
+        if level % 2:
+            pair = level // 2
+            for step in range(1, NL):
+                copy5(pair, step).wait_recv()
+            in5[0, pair] = out5[pair] + in5[1, pair] + in5[2, pair] + in5[3, pair]
+            for group in range(4):
+                at = pair * 2 * SL + group * 128
+                rows16[0:HZ, at : at + 128] = in5[0, pair, :, group, :]
+        shift = rows16[:, cols] + incoming
         out3[level, :, 0, :] = shift[:HZ, :128]
         out3[level, :, 1, :] = shift[:HZ, 128:]
         if level:
@@ -516,7 +527,8 @@
     for i in range(NZ - 1):
         copy2(i).wait_send()
     for step in range(1, NL):
-        copy5(step).wait_send()
+        copy5(0, step).wait_send()
+        copy5(1, step).wait_send()
         copy_l(step).wait_send()
     for one in straight + onward + onward_down:
         one.wait_send()
@@ -593,8 +605,8 @@
             pltpu.VMEM((NL, HZ, 2, 128), f32),
             pltpu.VMEM((HY, SL), f32),
             pltpu.VMEM((2 * HZ + 8, 128), f32),
-            pltpu.VMEM((HZ, 8, 128), f32),
-            pltpu.VMEM((NL, HZ, 8, 128), f32),
+            pltpu.VMEM((2, HZ, 4, 128), f32),
+            pltpu.VMEM((NL, 2, HZ, 4, 128), f32),
             pltpu.VMEM((NL, HZ, 2, 128), f32),
             pltpu.VMEM((NZ, HZ, 2, 128), f32),
             pltpu.VMEM((NZ, HZ, 2, 128), f32),
@@ -611,8 +623,8 @@
             dma((NZ,)),
             dma((len(PARTS),)),
             dma((len(PARTS),)),
-            dma((NL,)),
-            dma((NL,)),
+            dma((2, NL)),
+            dma((2, NL)),
             dma((NL,)),
             dma((NL,)),
             pltpu.SemaphoreType.REGULAR((2,)),

time: 53.1 us -> 52.2 us (0.983)
  Pallas kernels: 52.3 us -> 51.4 us
    pallas_call x1, Pallas kernels: 50.8 us -> 49.9 us  [local(): pl.pallas_call(kernel, name='prox', out_shape=(jax.ShapeDtypeStruct((HY,...]
where the time goes in v9:
time: 52.2 us; the launch traced here: 52.1 us
  Pallas kernels  51.4 us (98%)
  between operations  0.64 us (1%)
    pallas_call x1, Pallas kernels, local(): pl.pallas_call(kernel, name='prox', out_shape=(jax.ShapeDtypeStruct((HY,...  49.9 us
    pallas_call x1, Pallas kernels, local(): pl.pallas_call(last_pass, name='last_pass', out_shape=(jax.ShapeDtypeStru...  1.49 us

profile of v9, /device:TPU:10, one launch (start us, length us, event | category | flops | bytes accessed | tf_op | source)
XLA Modules:
  0.0 52.1 jit_solution(4328946357043338719)
XLA Ops:
  0.6 49.9 %prox.1 = (f32[192,256]{1,0:T(8,128)S(1)}, f32[192,256]{1,0:T(8,128)S(1)}, f32[192,256]{1,0:T(8,128)S(1)}, f32[8,256]{1,0:T(8,128)S(1)}, bf16[256,256]{1,0:T(8,128)(2,1)S(1)}) custom-call(bf16[3072,256]{1,0:T(8,128)(2,1)} %bitcast.1, bf16[256,1024]{1,0:T(8,128)(2,1)} %payoff.1, s32[8,5]{1,0:T(8,128)} %cards_hbm.1, s32[8,1326]{1,0:T(8,128)} %rank_hbm.1, ...), custom_call_target="tpu_custom_call" | custom-call | tf_op jit(solution)/shard_map/prox/pallas_call | solution.py:571
  50.6 1.5 %last_pass.1 = (f32[384,256]{1,0:T(8,128)}, f32[384,256]{1,0:T(8,128)}) custom-call(f32[192,256]{1,0:T(8,128)S(1)} %get-tuple-element.7.scores, f32[192,256]{1,0:T(8,128)S(1)} %get-tuple-element.8.own_policy, f32[192,256]{1,0:T(8,128)S(1)} %get-tuple-element.9.own_passed, f32[8,256]{1,0:T(8,128)S(1)} %get-tuple-element.10.legal, ...), custom_call_target="tpu_custom_call" | custom-call | tf_op jit(solution)/shard_map/last_pass/pallas_call | solution.py:652

commit v10 on v9

--- a/solution.py
+++ b/solution.py
@@ -135,7 +135,6 @@
     logit_tiles,
     logit_rows,
     total2,
-    halves,
     out5,
     in5,
     out3,
@@ -382,11 +381,11 @@
         for part in range(2):
             for from_y in range(2):
                 sums[part] += plane_rows(1 - part if late == 0 else part, from_y, part)
+    total2[HY:, :] = jnp.zeros((8, SL), jnp.float32)
     for part in range(2):
         total2[part * HH : part * HH + HH, :] = sums[part].astype(jnp.float32) * (SCALE_PLANE / SCALE)
     for to_z in range(NZ):
-        rows = total2[to_z * HZ : (to_z + 1) * HZ, :]
-        rows = jnp.round(jnp.concatenate([rows[:, :128], rows[:, 128:]], axis=0))
+        rows = jnp.round(total2[to_z * HZ : to_z * HZ + PAD, :])
         out2[to_z] = rows.astype(jnp.int32).astype(jnp.int16)
 
     pl.semaphore_wait(know.at[1], 2)
@@ -414,9 +413,7 @@
     for i in range(NZ - 2, -1, -1):
         copy2(i).wait_recv()
         total += in2[i].astype(jnp.int32)
-    halves[0 : 2 * HZ, :] = total.astype(jnp.float32)
-    halves[2 * HZ :, :] = jnp.zeros((8, 128), jnp.float32)
-    counter = jnp.concatenate([halves[0:PAD, :], halves[HZ : HZ + PAD, :]], axis=1)
+    counter = total.astype(jnp.float32)
     high = counter.astype(jnp.bfloat16).astype(jnp.float32)
     both = jnp.concatenate([high, counter - high], axis=0).astype(jnp.bfloat16)
 
@@ -596,15 +593,14 @@
             pltpu.VMEM((2, 2, HH, SL), i16),
             pltpu.VMEM((2, 2, HY, SL), i16),
             pltpu.VMEM((HY, SL), i16),
-            pltpu.VMEM((NZ, 2 * HZ, 128), i16),
-            pltpu.VMEM((NZ - 1, 2 * HZ, 128), i16),
+            pltpu.VMEM((NZ, PAD, SL), i16),
+            pltpu.VMEM((NZ - 1, PAD, SL), i16),
             pltpu.VMEM((PAD, SX), f32),
             pltpu.VMEM((PAD, SX), f32),
             pltpu.VMEM((SL, SX), bf16),
             pltpu.VMEM((HX, 2, 128), f32),
             pltpu.VMEM((NL, HZ, 2, 128), f32),
-            pltpu.VMEM((HY, SL), f32),
-            pltpu.VMEM((2 * HZ + 8, 128), f32),
+            pltpu.VMEM((HY + 8, SL), f32),
             pltpu.VMEM((2, HZ, 4, 128), f32),
             pltpu.VMEM((NL, 2, HZ, 4, 128), f32),
             pltpu.VMEM((NL, HZ, 2, 128), f32),

time: 52.2 us -> 52.9 us (1.013)
  Pallas kernels: 51.4 us -> 52.1 us
    pallas_call x1, Pallas kernels: 49.9 us -> 50.6 us  [local(): pl.pallas_call(kernel, name='prox', out_shape=(jax.ShapeDtypeStruct((HY,...]
where the time goes in v10:
time: 52.9 us; the launch traced here: 52.7 us
  Pallas kernels  52.1 us (98%)
  between operations  0.64 us (1%)
    pallas_call x1, Pallas kernels, local(): pl.pallas_call(kernel, name='prox', out_shape=(jax.ShapeDtypeStruct((HY,...  50.6 us
    pallas_call x1, Pallas kernels, local(): pl.pallas_call(last_pass, name='last_pass', out_shape=(jax.ShapeDtypeStru...  1.49 us

profile of v10, /device:TPU:10, one launch (start us, length us, event | category | flops | bytes accessed | tf_op | source)
XLA Modules:
  0.0 52.7 jit_solution(17376609410359906513)
XLA Ops:
  0.6 50.6 %prox.1 = (f32[192,256]{1,0:T(8,128)S(1)}, f32[192,256]{1,0:T(8,128)S(1)}, f32[192,256]{1,0:T(8,128)S(1)}, f32[8,256]{1,0:T(8,128)S(1)}, bf16[256,256]{1,0:T(8,128)(2,1)S(1)}) custom-call(bf16[3072,256]{1,0:T(8,128)(2,1)} %bitcast.1, bf16[256,1024]{1,0:T(8,128)(2,1)} %payoff.1, s32[8,5]{1,0:T(8,128)} %cards_hbm.1, s32[8,1326]{1,0:T(8,128)} %rank_hbm.1, ...), custom_call_target="tpu_custom_call" | custom-call | tf_op jit(solution)/shard_map/prox/pallas_call | solution.py:568
  51.2 1.5 %last_pass.1 = (f32[384,256]{1,0:T(8,128)}, f32[384,256]{1,0:T(8,128)}) custom-call(f32[192,256]{1,0:T(8,128)S(1)} %get-tuple-element.7.scores, f32[192,256]{1,0:T(8,128)S(1)} %get-tuple-element.8.own_policy, f32[192,256]{1,0:T(8,128)S(1)} %get-tuple-element.9.own_passed, f32[8,256]{1,0:T(8,128)S(1)} %get-tuple-element.10.legal, ...), custom_call_target="tpu_custom_call" | custom-call | tf_op jit(solution)/shard_map/last_pass/pallas_call | solution.py:648
